TPU v7x, 512 devices: a whole 4x4x16 slice. The times are simulated.
512 devices in a mesh: section: 16 (over y, x), tp: 32 (over z, core).
Axes of the slice: x: 4, y: 4, z: 16, core: 2. Of those that a mesh axis runs over, the one named last changes fastest.
Arguments:
- hidden: bfloat16 [16, 128, 8192], P('section', 'tp'), may hold values from -6 to 6
- norm_gain: float32 [16, 8192], P('section'), may hold values from 0.25 to 1.75
- q_gain: float32 [16, 8192], P('section'), may hold values from 0.1 to 40, as said below
- out_weight: bfloat16 [16, 8192, 8192], P('section', 'tp'), may hold values from -0.0625 to 0.0625
- positions: int32 [16, 128], P('section'), may hold values from 0 to 127, as said below
Outputs:
- advanced: bfloat16 [16, 128, 8192], P('section', 'tp')
Inputs may be any that keep to these rules, and one draw needn't show every extreme that they name: `q_gain`: positive gains; in each layer some heads' gains may be several times larger than the others'. `positions`: each micro-batch is a run of whole documents: position 0 starts a document and each next token's position is one more; one micro-batch of every draw is a single document.
All inputs are finite; a program needn't handle non-finite values. Where the computation divides by a largest or mean magnitude, that divisor is 1e-20 or more.
Results may differ from a plain program's by a relative error of at most 0.03.
Values may be sent and summed in bfloat16 or wider, within the bound.
A program may use at most 64 MiB of HBM per device.

v0:
```python
import jax
import jax.numpy as jnp
from jax import lax
from jax.sharding import PartitionSpec as P

HEAD = 128
BLOCK = 128
TICKS = 2


code_limit = 3.0


def from_behind(value, axis, steps):
    count = lax.axis_size(axis)
    pairs = [(source, (source + steps) % count) for source in range(count)]
    return lax.ppermute(value, axis, pairs)


def sign_table(width):
    rows = lax.broadcasted_iota(jnp.int32, (width, width), 0)
    cols = lax.broadcasted_iota(jnp.int32, (width, width), 1)
    both = jnp.bitwise_and(rows, cols)
    parity = jnp.zeros((width, width), jnp.int32)
    for place in range(width.bit_length() - 1):
        parity = parity + jnp.bitwise_and(jnp.right_shift(both, place), 1)
    return (1 - 2 * jnp.bitwise_and(parity, 1)).astype(jnp.float32)


def normalize(state, gain):
    flat = state.astype(jnp.float32)
    meansq = jnp.mean(flat * flat, axis=-1, keepdims=True)
    return (flat * lax.rsqrt(meansq + 1e-05) * gain).astype(jnp.bfloat16)


def attend(columns, qcols, pos):
    tokens = columns.shape[0]
    local = columns.shape[1]
    heads_here = local // HEAD
    keys = columns.reshape(tokens, heads_here, HEAD)
    query = (keys.astype(jnp.float32) * qcols.reshape(heads_here, HEAD)).astype(jnp.bfloat16)
    scores = jnp.einsum("thd,shd->hts", query, keys, preferred_element_type=jnp.float32) * HEAD ** (
        -0.5
    )
    row_ids = lax.broadcasted_iota(jnp.int32, (tokens, tokens), 0)
    col_ids = lax.broadcasted_iota(jnp.int32, (tokens, tokens), 1)
    seen = (col_ids <= row_ids) & (col_ids >= row_ids - pos[:, None])
    scores = jnp.where(seen[None], scores, -1e30)
    top = jnp.max(scores, axis=-1, keepdims=True)
    expo = jnp.where(seen[None], jnp.exp(scores - top), 0.0)
    weights = (expo / jnp.sum(expo, axis=-1, keepdims=True)).astype(jnp.bfloat16)
    context = jnp.einsum("hts,shd->thd", weights, keys, preferred_element_type=jnp.float32)
    return context.astype(jnp.bfloat16).reshape(tokens, local)


def encode(partial_value, table):
    tokens = partial_value.shape[0]
    width = partial_value.shape[1]
    pieces = partial_value.reshape(tokens, width // BLOCK, BLOCK)
    rotated = jnp.einsum("tbk,kj->tbj", pieces, table, preferred_element_type=jnp.float32)
    scale = jnp.mean(jnp.abs(rotated), axis=-1) + 1e-06
    coded = jnp.clip(rotated / scale[..., None], -code_limit, code_limit).astype(jnp.bfloat16)
    return (coded.reshape(tokens, width), scale)


def combine_terms(received):
    coded, scale = received
    sources = coded.shape[0]
    count = coded.shape[2]
    width = coded.shape[3]
    terms = (
        coded.astype(jnp.float32).reshape(sources, count, width // BLOCK, BLOCK)
        * scale[0:sources, 0][..., None]
    )
    return jnp.sum(terms, axis=0).reshape(count, width)


def recode(summed):
    count = summed.shape[0]
    width = summed.shape[1]
    pieces = summed.reshape(count, width // BLOCK, BLOCK)
    rescale = jnp.mean(jnp.abs(pieces), axis=-1) + 1e-06
    recoded = jnp.clip(pieces / rescale[..., None], -code_limit, code_limit).astype(jnp.bfloat16)
    return (recoded.reshape(count, width), rescale)


def restore(recoded, rescale, table):
    count = recoded.shape[0]
    width = recoded.shape[1]
    pieces = recoded.reshape(count, width // BLOCK, BLOCK)
    back = jnp.einsum("tbk,kj->tbj", pieces, table, preferred_element_type=jnp.float32)
    back = back * (rescale / BLOCK)[..., None]
    return back.reshape(count, width)


def per_device(hidden, norm_gain, q_gain, out_weight, positions):
    groups = lax.axis_size("tp")
    member = lax.axis_index("tp")
    owned = hidden.shape[1]
    local = out_weight.shape[1]
    gain = norm_gain[0]
    qcols = lax.dynamic_slice_in_dim(q_gain[0], member * local, local, 0)
    weight = out_weight[0]
    pos = positions[0]
    table = sign_table(BLOCK).astype(jnp.bfloat16)
    state_full = lax.all_gather(hidden[0], "tp", axis=0, tiled=True)
    for tick in range(TICKS):
        tokens = state_full.shape[0]
        width = state_full.shape[1]
        normed = normalize(state_full, gain)
        columns = lax.dynamic_slice_in_dim(normed, member * local, local, 1)
        context = attend(columns, qcols, pos)
        partial_value = jnp.dot(context, weight, preferred_element_type=jnp.float32).astype(
            jnp.bfloat16
        )
        coded, scale = encode(partial_value, table)
        coded_split = coded.reshape(1, groups, tokens // groups, width)
        scale_split = scale.reshape(1, groups, tokens // groups, width // BLOCK)
        summed = combine_terms(
            (
                lax.all_to_all(coded_split, "tp", split_axis=1, concat_axis=0, tiled=True),
                lax.all_to_all(
                    scale_split.astype(jnp.bfloat16), "tp", split_axis=1, concat_axis=0, tiled=True
                ).astype(scale_split.dtype),
            )
        )
        recoded, rescale = recode(summed)
        recoded_all, rescale_all = (
            lax.all_gather(recoded, "tp", axis=0, tiled=True),
            lax.all_gather(rescale.astype(jnp.bfloat16), "tp", axis=0, tiled=True).astype(
                rescale.dtype
            ),
        )
        state_full = (
            state_full.astype(jnp.float32) + restore(recoded_all, rescale_all, table)
        ).astype(jnp.bfloat16)
        state_full, pos = from_behind((state_full, pos), "section", 1)
    result = lax.dynamic_slice_in_dim(state_full, member * owned, owned, 0)
    return result[None]


def solution(mesh):
    return jax.shard_map(
        per_device,
        mesh=mesh,
        in_specs=(
            P("section", "tp", None),
            P("section", None),
            P("section", None),
            P("section", "tp", None),
            P("section", None),
        ),
        out_specs=P("section", "tp", None),
        check_vma=False,
    )
```

profile of v0, /device:TPU:1, one launch (start us, length us, event | category | flops | bytes accessed | tf_op | source)
XLA Modules:
  0.0 650.9 jit_solution(7665034053108164784)
XLA Ops:
  9.6 79.4 %all-gather.9.cloned.1.call-done = bf16[1,128,8192]{2,0,1:T(2,128)(2,1)} async-done(((bf16[1,4,8192]{2,0,1:T(2,128)(2,1)}), bf16[1,128,8192]{2,0,1:T(2,128)(2,1)}) %all-gather.9.cloned.1.call-update) | async-done | bytes 2097168 | tf_op jit(solution)/shard_map/all_gather | solution.py:106
  89.0 8.8 %copy.53 = bf16[1,128,8192]{1,2,0:T(8,128)(2,1)S(1)} copy(bf16[1,128,8192]{2,0,1:T(2,128)(2,1)} %all-gather.9.cloned.1.call-done) | data formatting | bytes 4194304 | tf_op jit(solution)/shard_map/all_gather | solution.py:106
  106.2 8.4 %all-to-all-start.1 = ((bf16[32,2,128]{2,1,0:T(2,128)(2,1)}), bf16[32,2,128]{2,1,0:T(2,128)(2,1)S(1)}, u32[]{:S(2)}, u32[]{:S(2)}) async-start(bf16[32,2,128]{2,1,0:T(2,128)(2,1)} %reshape.280), calls=%async_computation.1 | async-start | bytes 32768 | tf_op jit(solution)/shard_map/all_to_all | solution.py:122
  114.6 4.2 clamp_convert_fusion.1
  118.8 4.1 copy.58
  127.0 12.2 %all-to-all-start = ((bf16[1,32,4,8192]{3,2,0,1:T(4,128)(2,1)}), bf16[1,32,4,8192]{3,2,0,1:T(4,128)(2,1)}, u32[]{:S(2)}, u32[]{:S(2)}) async-start(bf16[1,32,4,8192]{3,2,0,1:T(4,128)(2,1)} %bitcast.127), calls=%async_computation | async-start | bytes 4194304 | tf_op jit(solution)/shard_map/all_to_all | solution.py:121
  141.9 5.5 mul.136
  147.4 90.4 %all-to-all-done = bf16[1,32,4,8192]{3,2,0,1:T(4,128)(2,1)} async-done(((bf16[1,32,4,8192]{3,2,0,1:T(4,128)(2,1)}), bf16[1,32,4,8192]{3,2,0,1:T(4,128)(2,1)}, u32[]{:S(2)}, u32[]{:S(2)}) %all-to-all-start) | async-done | bytes 2097184 | tf_op jit(solution)/shard_map/all_to_all | solution.py:121
  237.8 4.1 multiply_reduce_fusion.2
  243.0 30.2 %all-gather.2 = bf16[32,4,64]{2,1,0:T(4,128)(2,1)S(1)} all-gather(bf16[1,4,64]{2,1,0:T(4,128)(2,1)S(1)} %get-tuple-element.11), channel_id=1, replica_groups=mesh['section'=16,'tp'=32] {'tp'}, dimensions={0}, use_global_device_ids=true | all-gather | bytes 16896 | tf_op jit(solution)/shard_map/all_gather | solution.py:130
  273.2 35.7 %all-gather.11.cloned.1.call-done = bf16[32,4,8192]{2,1,0:T(4,128)(2,1)} async-done(((bf16[1,4,8192]{2,1,0:T(4,128)(2,1)}), bf16[32,4,8192]{2,1,0:T(4,128)(2,1)}) %all-gather.11.cloned.1.call-update) | async-done | bytes 2097168 | tf_op jit(solution)/shard_map/all_gather | solution.py:129
  308.9 4.8 reshape.252
  323.8 45.8 %collective-permute-done.1 = s32[128]{0:T(128)S(1)} collective-permute-done((s32[128]{0:T(128)S(1)}, s32[128]{0:T(128)S(1)}, u32[]{:S(2)}, u32[]{:S(2)}) %collective-permute-start.1) | collective-permute-done | bytes 544 | tf_op jit(solution)/shard_map/ppermute | solution.py:17
  378.1 9.1 %all-to-all-start.3 = ((bf16[32,2,128]{2,1,0:T(2,128)(2,1)}), bf16[32,2,128]{2,1,0:T(2,128)(2,1)S(1)}, u32[]{:S(2)}, u32[]{:S(2)}) async-start(bf16[32,2,128]{2,1,0:T(2,128)(2,1)} %reshape.282), calls=%async_computation.3 | async-start | bytes 32768 | tf_op jit(solution)/shard_map/all_to_all | solution.py:122
  387.2 4.2 clamp_convert_fusion
  391.4 4.1 copy.68
  399.6 12.2 %all-to-all-start.2 = ((bf16[1,32,4,8192]{3,2,0,1:T(4,128)(2,1)}), bf16[1,32,4,8192]{3,2,0,1:T(4,128)(2,1)}, u32[]{:S(2)}, u32[]{:S(2)}) async-start(bf16[1,32,4,8192]{3,2,0,1:T(4,128)(2,1)} %bitcast.128), calls=%async_computation.2 | async-start | bytes 4194304 | tf_op jit(solution)/shard_map/all_to_all | solution.py:121
  414.5 5.5 mul.147
  420.0 90.4 %all-to-all-done.2 = bf16[1,32,4,8192]{3,2,0,1:T(4,128)(2,1)} async-done(((bf16[1,32,4,8192]{3,2,0,1:T(4,128)(2,1)}), bf16[1,32,4,8192]{3,2,0,1:T(4,128)(2,1)}, u32[]{:S(2)}, u32[]{:S(2)}) %all-to-all-start.2) | async-done | bytes 2097184 | tf_op jit(solution)/shard_map/all_to_all | solution.py:121
  510.4 4.1 multiply_reduce_fusion
  515.6 30.2 %all-gather.4 = bf16[32,4,64]{2,1,0:T(4,128)(2,1)S(1)} all-gather(bf16[1,4,64]{2,1,0:T(4,128)(2,1)S(1)} %get-tuple-element.9), channel_id=1, replica_groups=mesh['section'=16,'tp'=32] {'tp'}, dimensions={0}, use_global_device_ids=true | all-gather | bytes 16896 | tf_op jit(solution)/shard_map/all_gather | solution.py:130
  545.9 32.3 %all-gather.13.cloned.1.call-done = bf16[32,4,8192]{2,1,0:T(4,128)(2,1)} async-done(((bf16[1,4,8192]{2,1,0:T(4,128)(2,1)}), bf16[32,4,8192]{2,1,0:T(4,128)(2,1)}) %all-gather.13.cloned.1.call-update) | async-done | bytes 2097168 | tf_op jit(solution)/shard_map/all_gather | solution.py:129
  578.1 4.8 reshape.257
  591.3 49.4 %collective-permute-done.2 = bf16[128,8192]{0,1:T(8,128)(2,1)} collective-permute-done((bf16[128,8192]{0,1:T(8,128)(2,1)}, bf16[128,8192]{0,1:T(8,128)(2,1)}, u32[]{:S(2)}, u32[]{:S(2)}) %collective-permute-start.2) | collective-permute-done | bytes 2097184 | tf_op jit(solution)/shard_map/ppermute | solution.py:17
  (77 shorter events, 57.8 us)
Async XLA Ops:
  6.5 2.4 copy-start
  6.5 82.4 %all-gather.9.cloned.1.call-start = ((), (), s32[]{:S(2)}) async-start(), calls=%async_computation.4 | async-start | bytes 4325376 | tf_op jit(solution)/shard_map/all_gather | solution.py:106
  106.2 20.7 %all-to-all-start.1 = ((bf16[32,2,128]{2,1,0:T(2,128)(2,1)}), bf16[32,2,128]{2,1,0:T(2,128)(2,1)S(1)}, u32[]{:S(2)}, u32[]{:S(2)}) async-start(bf16[32,2,128]{2,1,0:T(2,128)(2,1)} %reshape.280), calls=%async_computation.1 | async-start | bytes 32768 | tf_op jit(solution)/shard_map/all_to_all | solution.py:122
  127.0 110.9 %all-to-all-start = ((bf16[1,32,4,8192]{3,2,0,1:T(4,128)(2,1)}), bf16[1,32,4,8192]{3,2,0,1:T(4,128)(2,1)}, u32[]{:S(2)}, u32[]{:S(2)}) async-start(bf16[1,32,4,8192]{3,2,0,1:T(4,128)(2,1)} %bitcast.127), calls=%async_computation | async-start | bytes 4194304 | tf_op jit(solution)/shard_map/all_to_all | solution.py:121
  139.2 169.7 %all-gather.11.cloned.1.call-start = ((), (), s32[]{:S(2)}) async-start(), calls=%async_computation.5 | async-start | bytes 2162688 | tf_op jit(solution)/shard_map/all_gather | solution.py:129
  317.0 3.5 copy-start.2
  317.4 52.2 %collective-permute-start = (bf16[128,8192]{0,1:T(8,128)(2,1)S(1)}, bf16[128,8192]{0,1:T(8,128)(2,1)S(1)}, u32[]{:S(2)}, u32[]{:S(2)}) collective-permute-start(bf16[128,8192]{0,1:T(8,128)(2,1)S(1)} %fusion.3), channel_id=1, source_target_pairs={{0,32},{32,64},{64,96},{96,128},{128,160},{160,192},{192,224},{224... | collective-permute-start | bytes 6291464 | tf_op jit(solution)/shard_map/ppermute | solution.py:17
  320.6 49.1 %collective-permute-start.1 = (s32[128]{0:T(128)S(1)}, s32[128]{0:T(128)S(1)}, u32[]{:S(2)}, u32[]{:S(2)}) collective-permute-start(s32[128]{0:T(128)S(1)} %bitcast.142), channel_id=1, source_target_pairs={{0,32},{32,64},{64,96},{96,128},{128,160},{160,192},{192,224},{224... | collective-permute-start | bytes 1544 | tf_op jit(solution)/shard_map/ppermute | solution.py:17
  378.1 21.4 %all-to-all-start.3 = ((bf16[32,2,128]{2,1,0:T(2,128)(2,1)}), bf16[32,2,128]{2,1,0:T(2,128)(2,1)S(1)}, u32[]{:S(2)}, u32[]{:S(2)}) async-start(bf16[32,2,128]{2,1,0:T(2,128)(2,1)} %reshape.282), calls=%async_computation.3 | async-start | bytes 32768 | tf_op jit(solution)/shard_map/all_to_all | solution.py:122
  399.6 110.9 %all-to-all-start.2 = ((bf16[1,32,4,8192]{3,2,0,1:T(4,128)(2,1)}), bf16[1,32,4,8192]{3,2,0,1:T(4,128)(2,1)}, u32[]{:S(2)}, u32[]{:S(2)}) async-start(bf16[1,32,4,8192]{3,2,0,1:T(4,128)(2,1)} %bitcast.128), calls=%async_computation.2 | async-start | bytes 4194304 | tf_op jit(solution)/shard_map/all_to_all | solution.py:121
  411.8 166.3 %all-gather.13.cloned.1.call-start = ((), (), s32[]{:S(2)}) async-start(), calls=%async_computation.6 | async-start | bytes 2162688 | tf_op jit(solution)/shard_map/all_gather | solution.py:129
  586.2 58.2 %copy-start.1 = (f32[1,8192]{1,0:T(1,128)S(1)}, f32[1,8192]{1,0:T(1,128)}, u32[]{:S(2)}) copy-start(f32[1,8192]{1,0:T(1,128)} %param.7) | copy-start | bytes 98308
  588.1 52.5 %collective-permute-start.2 = (bf16[128,8192]{0,1:T(8,128)(2,1)}, bf16[128,8192]{0,1:T(8,128)(2,1)}, u32[]{:S(2)}, u32[]{:S(2)}) collective-permute-start(bf16[128,8192]{0,1:T(8,128)(2,1)} %fusion.2), channel_id=1, source_target_pairs={{0,32},{32,64},{64,96},{96,128},{128,160},{160,192},{192,224},{224... | collective-permute-start | bytes 6291464 | tf_op jit(solution)/shard_map/ppermute | solution.py:17
Sparse Core Ops, SparseCore 0:
  9.5 79.4 all-gather.8
  243.1 65.7 all-gather.10
  515.7 62.3 all-gather.12
where the time goes:
time: 652 us; the launch traced here: 651 us
  waiting for transfers between devices  423 us (65%)
  blocking collectives  60.4 us (9%)
  local copies, waits for them, and re-layouts  59.1 us (9%)
  starting transfers between devices  51.4 us (8%)
  other arithmetic  24.5 us (4%)
  matrix products  18.7 us (3%)
  between operations  13.4 us (2%)
    all_to_all x2, waiting for transfers between devices, per_device(): lax.all_to_all(coded_split, 'tp', split_axis=1, concat_axis=0, tiled=True)  181 us
    ppermute x3, waiting for transfers between devices, from_behind(): return lax.ppermute(value, axis, pairs)  95.2 us
    all_gather x1, waiting for transfers between devices, per_device(): state_full = lax.all_gather(hidden[0], 'tp', axis=0, tiled=True)  79.4 us
    all_gather x2, waiting for transfers between devices, per_device(): lax.all_gather(recoded, 'tp', axis=0, tiled=True)  67.9 us
    all_gather x2, blocking collectives, per_device(): lax.all_gather(rescale.astype(jnp.bfloat16), 'tp', axis=0, tiled=True)  60.4 us
    all_to_all x2, starting transfers between devices, per_device(): lax.all_to_all(coded_split, 'tp', split_axis=1, concat_axis=0, tiled=True)  24.5 us
    all_to_all x2, starting transfers between devices, per_device(): lax.all_to_all(scale_split.astype(jnp.bfloat16), 'tp', split_axis=1, conc...  17.4 us
    mul x4, local copies, waits for them, and re-layouts, combine_terms(): coded.astype(jnp.float32).reshape(sources, count, width // BLOCK, BLOCK)  16.1 us
  transfers between devices with their start and end apart: 10, of which 7 were waited for; matrix products, arithmetic and copies ran while one was open for 7% of the time, Pallas kernels for 0%

commit v1 on v0

v1 whole, which is shorter than its diff:
```python
import jax
import jax.numpy as jnp
from jax import lax
from jax.experimental import pallas as pl
from jax.experimental.pallas import tpu as pltpu
from jax.sharding import PartitionSpec as P

MESH = pl.DeviceIdType.MESH
F32 = jnp.float32
BF16 = jnp.bfloat16
HEAD = 128
BLOCK = 128
TICKS = 2
LIMIT = 3.0
NZ = 16
TILE = 256
TOK = 128
ROWS = 8
HALF = 2048
NSUB = 4
PART = HALF // NSUB


def constants():
    rows = lax.broadcasted_iota(jnp.int32, (TILE, TILE), 0)
    cols = lax.broadcasted_iota(jnp.int32, (TILE, TILE), 1)
    same = jnp.right_shift(rows, 7) == jnp.right_shift(cols, 7)
    both = jnp.bitwise_and(rows, cols)
    for shift in (4, 2, 1):
        both = jnp.bitwise_xor(both, jnp.right_shift(both, shift)) if shift != 4 else jnp.bitwise_xor(
            jnp.bitwise_and(both, 15), jnp.bitwise_and(jnp.right_shift(both, 4), 7)
        )
    sign = (1 - 2 * jnp.bitwise_and(both, 1)).astype(F32)
    signs = jnp.where(same, sign, 0.0).astype(BF16)
    means = jnp.where(same, 1.0 / BLOCK, 0.0).astype(BF16)
    return signs, means


def swap(p, q):
    low = lax.broadcasted_iota(jnp.int32, p.shape, 0) < 4
    return (
        jnp.where(low, p, pltpu.roll(q, 4, 0)),
        jnp.where(low, pltpu.roll(p, 4, 0), q),
    )


def dot(a, b):
    return jnp.dot(a, b, preferred_element_type=F32)


def kernel(
    hidden, gain, qgain, weight, pos, out,
    signs, means, x8, st, wb, msb, mrb, gbuf, pbuf, asb, arb, cbuf, terms, sb, rb, ssb, srb, rsb, rrb, fsb, frb,
    wsem, wss, wrs, mss, mrs, ass, ars, css, crs, rss, rrs, fss, frs,
):
    sec = lax.axis_index("section")
    tp = lax.axis_index("tp")
    nsec = lax.axis_size("section")
    z = tp // 2
    k = lax.rem(tp, 2)
    sib = (sec, z * 2 + 1 - k)
    nxt = lax.rem(sec + 1, nsec)
    prv = lax.rem(sec + nsec - 1, nsec)

    def far(i):
        return lax.rem(z + i, NZ)

    def remote(src, dst, send, recv, device):
        return pltpu.make_async_remote_copy(
            src_ref=src, dst_ref=dst, send_sem=send, recv_sem=recv, device_id=device, device_id_type=MESH
        )

    def wcols(jj, parity):
        return pl.ds(pl.multiple_of((2 * jj + parity) * TILE, TILE), TILE)

    def wlocal(jj):
        return pltpu.make_async_copy(weight.at[0, :, wcols(jj, k)], wb.at[0, jj], wsem.at[jj])

    def wremote(jj):
        return remote(weight.at[0, :, wcols(jj, 1 - k)], wb.at[1, jj], wss.at[jj], wrs.at[jj], sib)

    def loop(n, body):
        lax.fori_loop(0, n, lambda i, c: (body(i), c)[1], 0)

    loop(NZ, lambda jj: wlocal(jj).start())

    barrier = pltpu.get_barrier_semaphore()

    def greet(section, member):
        pl.semaphore_signal(barrier, inc=1, device_id=(section, member), device_id_type=MESH)

    def greet_far(i):
        greet(sec, far(i) * 2 + k)
        greet(prv, far(i) * 2 + k)

    greet(*sib)
    lax.fori_loop(1, NZ, lambda i, c: (greet_far(i), c)[1], 0)
    greet(prv, z * 2 + k)
    greet(prv, z * 2 + 1 - k)
    greet(nxt, z * 2 + k)

    sg, mn = constants()
    signs[...] = sg
    means[...] = mn

    x = hidden[0].astype(F32)
    x8[0:4, :] = x
    x8[4:8, :] = x
    x = x8[...]
    scale = lax.rsqrt(jnp.mean(x * x, axis=1, keepdims=True) + 1e-05)
    normed = x * scale * gain[...]

    def pack(v, parity):
        quarters = []
        for q in range(4):
            quarters.append(
                jnp.concatenate(
                    [v[:, (2 * jj + parity) * TILE : (2 * jj + parity + 1) * TILE] for jj in range(4 * q, 4 * q + 4)],
                    axis=1,
                )
            )
        return jnp.concatenate([swap(quarters[0], quarters[1])[0], swap(quarters[2], quarters[3])[0]], axis=0)

    even = k == 0
    for i, v in enumerate((normed, x)):
        p0, p1 = pack(v, 0), pack(v, 1)
        msb[i] = jnp.where(even, p0, p1).astype(BF16)
        msb[2 + i] = jnp.where(even, p1, p0).astype(BF16)

    pl.semaphore_wait(barrier, 2 * NZ + 2)

    packs = [remote(msb.at[2 + i], mrb.at[i], mss.at[i], mrs.at[i], sib) for i in range(2)]
    for c in packs:
        c.start()
    loop(NZ, lambda jj: wremote(jj).start())
    gains = remote(gain, gbuf, mss.at[2], mrs.at[2], (prv, z * 2 + k))
    gains.start()
    places = remote(pos, pbuf, mss.at[3], mrs.at[3], (nxt, z * 2 + k))
    places.start()

    def unpack(i):
        mine, other = msb[i].astype(F32), mrb[i].astype(F32)
        a = jnp.where(even, mine, other)
        b = jnp.where(even, other, mine)
        halves = [jnp.concatenate(swap(a[8 * h : 8 * h + 8], b[8 * h : 8 * h + 8]), axis=1) for h in range(2)]
        return jnp.concatenate(halves, axis=0)

    def a2a_copy(tick, i):
        j = far(i)
        return remote(
            asb.at[tick, j], arb.at[tick, z], ass.at[tick, j], ars.at[tick, z],
            (sec if tick == 0 else nxt, j * 2 + k),
        )

    def a2a_recv(tick, i):
        j = far(i)
        return remote(asb.at[tick, j], arb.at[tick, j], ass.at[tick, j], ars.at[tick, j], (sec, j * 2 + k))

    def spread(tick, rows):
        for jj in range(NZ):
            h, c = jj // 8, (jj % 8) * TILE
            asb[tick, jj] = jnp.concatenate(
                [rows[8 * h : 8 * h + 8, c : c + HEAD], rows[8 * h : 8 * h + 8, c + HEAD : c + 2 * HEAD]], axis=0
            ).astype(BF16)
        lax.fori_loop(0 if tick else 1, NZ, lambda i, c: (a2a_copy(tick, lax.rem(i + 8, NZ) if tick else i).start(), c)[1], 0)
        if tick == 0:
            arb[0, z] = asb[0, z]

    packs[0].wait_recv()
    spread(0, unpack(0))
    packs[1].wait_recv()
    st[...] = unpack(1)

    def rotate(g):
        def one(jj):
            if g == 0:
                wlocal(jj).wait()
            else:
                wremote(jj).wait_recv()
            wb[g, jj] = dot(wb[g, jj], signs[...]).astype(BF16)

        loop(NZ, one)

    rotate(0)
    rotate(1)

    def attend(tick):
        rid = lax.broadcasted_iota(jnp.int32, (TOK, TOK), 0)
        cid = lax.broadcasted_iota(jnp.int32, (TOK, TOK), 1)
        row = (pos if tick == 0 else pbuf)[...].astype(F32)
        back = jnp.sum(jnp.where(rid == cid, jnp.broadcast_to(row, (TOK, TOK)), 0.0), axis=1, keepdims=True)
        seen = (cid <= rid) & (cid.astype(F32) >= rid.astype(F32) - back)
        lax.fori_loop(0 if tick else 1, NZ, lambda i, c: (a2a_recv(tick, i).wait_recv(), c)[1], 0)
        v = arb[tick].astype(F32).reshape(NZ, 2, ROWS, HEAD)
        for h in range(2):
            keys = v[:, h].reshape(TOK, HEAD)
            qg = qgain[:, pl.ds(pl.multiple_of(tp * TILE + h * HEAD, HEAD), HEAD)]
            query = (keys * qg).astype(BF16)
            keys = keys.astype(BF16)
            scores = lax.dot_general(query, keys, (((1,), (1,)), ((), ())), preferred_element_type=F32) * HEAD ** (-0.5)
            scores = jnp.where(seen, scores, -1e30)
            top = jnp.max(scores, axis=1, keepdims=True)
            expo = jnp.where(seen, jnp.exp(scores - top), 0.0)
            weights = (expo / jnp.sum(expo, axis=1, keepdims=True)).astype(BF16)
            cbuf[tick, 0, :, h * HEAD : (h + 1) * HEAD] = dot(weights, keys).astype(BF16)

    def part_terms(tick, j):
        for h in range(2):
            for i in range(PART // TILE):
                jj = h * 8 + j * (PART // TILE) + i
                total = None
                for g in range(2):
                    rotated = dot(cbuf[tick, g], wb[g, jj])
                    bound = dot(jnp.abs(rotated).astype(BF16), means[...]) * LIMIT + LIMIT * 1e-06
                    term = jnp.clip(rotated, -bound, bound)
                    total = term if total is None else total + term
                terms[:, h * 8 : h * 8 + 8, j * PART + i * TILE : j * PART + (i + 1) * TILE] = total.reshape(NZ, ROWS, TILE)

    def chain(tick, t, d, j):
        cols = pl.ds(j * PART, PART)
        to = (sec, far(1 if d == 0 else NZ - 1) * 2 + k)
        return remote(
            sb.at[tick, t, d, :, cols], rb.at[tick, t, d, :, cols], rss.at[tick, t, d, j], rrs.at[tick, t, d, j], to
        )

    def starts(t, d, j):
        return t == 0 or (t == 1 and j % 2 != d)

    def reduce(tick):
        for t in range(8):
            for j in range(NSUB):
                if t == 0:
                    part_terms(tick, j)
                cols = slice(j * PART, (j + 1) * PART)
                for d in range(2):
                    if t == 0 and j % 2 != d:
                        continue
                    owner = far(8 - t if d == 0 else 8 + t)
                    v = terms[owner, :, cols]
                    if not starts(t, d, j):
                        chain(tick, t - 1, d, j).wait_recv()
                        v = v + rb[tick, t - 1, d, :, cols].astype(F32)
                    sb[tick, t, d, :, cols] = v.astype(BF16)
                    chain(tick, t, d, j).start()
        sums = []
        for j in range(NSUB):
            cols = slice(j * PART, (j + 1) * PART)
            for d in range(2):
                chain(tick, 7, d, j).wait_recv()
            sums.append(terms[z, :, cols] + rb[tick, 7, 0, :, cols].astype(F32) + rb[tick, 7, 1, :, cols].astype(F32))
        summed = jnp.concatenate(sums, axis=1)
        n = HALF // BLOCK
        tall = jnp.concatenate([summed[:, b * BLOCK : (b + 1) * BLOCK] for b in range(n)], axis=0)
        rescale = jnp.mean(jnp.abs(tall), axis=1, keepdims=True) + 1e-06
        recoded = jnp.clip(tall / rescale, -LIMIT, LIMIT).astype(BF16)
        back = dot(recoded, signs[0:BLOCK, 0:BLOCK]) * (rescale / BLOCK)
        wide = jnp.concatenate([back[b * 16 : (b + 1) * 16] for b in range(n)], axis=1)
        return (st[...] + wide).astype(BF16)

    for tick in range(TICKS):
        attend(tick)
        swapc = remote(cbuf.at[tick, 0], cbuf.at[tick, 1], css.at[tick], crs.at[tick], sib)
        swapc.start()
        swapc.wait_recv()
        rows = reduce(tick)
        if tick == 0:
            state = rows.astype(F32)
            rsb[...] = rows
            part = jnp.sum(state * state, axis=1, keepdims=True)
            part = part[0:8] + part[8:16]
            ssb[...] = jnp.broadcast_to(part, (ROWS, BLOCK))
            sums = remote(ssb, srb, mss.at[4], mrs.at[4], sib)
            sums.start()
            residual = remote(rsb, rrb, mss.at[5], mrs.at[5], (nxt, z * 2 + k))
            residual.start()
            gains.wait_recv()
            cut = [gbuf[:, wcols(jj, k)] for jj in range(NZ)]
            sums.wait_recv()
            scale = lax.rsqrt((ssb[:, 0:1] + srb[:, 0:1]) / (2.0 * 2 * HALF) + 1e-05)
            halves = [
                state[8 * h : 8 * h + 8] * scale * jnp.concatenate(cut[8 * h : 8 * h + 8], axis=1) for h in range(2)
            ]
            spread(1, jnp.concatenate(halves, axis=0))
            places.wait_recv()
            residual.wait_recv()
            st[...] = rrb[...].astype(F32)
        else:
            v = rows.astype(F32)
            pair = [swap(v[8 * h : 8 * h + 8, 0:1024], v[8 * h : 8 * h + 8, 1024:2048]) for h in range(2)]
            for c in range(2):
                fsb[c] = jnp.concatenate([pair[0][c], pair[1][c]], axis=0).astype(BF16)

    def final(c):
        return remote(fsb.at[c], frb.at[k], fss.at[c], frs.at[k], (nxt, z * 2 + c))

    for c in range(2):
        final(c).start()
    for c in range(2):
        remote(fsb.at[c], frb.at[c], fss.at[c], frs.at[c], (nxt, z * 2 + c)).wait_recv()
    got = [frb[c].astype(F32) for c in range(2)]
    pieces = []
    for jj in range(NZ):
        q, c0 = jj // 4, (jj % 4) * TILE
        for c in range(2):
            v = got[c][8 * (q // 2) : 8 * (q // 2) + 8, c0 : c0 + TILE]
            pieces.append(pltpu.roll(v, 4, 0) if q % 2 else v)
    out[0] = jnp.concatenate(pieces, axis=1)[0:4].astype(BF16)

    for c in packs + [gains, places, sums, residual]:
        c.wait_send()
    loop(NZ, lambda jj: wremote(jj).wait_send())
    for tick in range(TICKS):
        lax.fori_loop(0 if tick else 1, NZ, lambda i, c: (a2a_copy(tick, i).wait_send(), c)[1], 0)
        remote(cbuf.at[tick, 0], cbuf.at[tick, 1], css.at[tick], crs.at[tick], sib).wait_send()
        for t in range(8):
            for j in range(NSUB):
                for d in range(2):
                    if t == 0 and j % 2 != d:
                        continue
                    chain(tick, t, d, j).wait_send()
    for c in range(2):
        final(c).wait_send()


def per_device(hidden, norm_gain, q_gain, out_weight, positions):
    vmem = pl.BlockSpec(memory_space=pltpu.VMEM)
    dma = pltpu.SemaphoreType.DMA
    return pl.pallas_call(
        kernel,
        out_shape=jax.ShapeDtypeStruct(hidden.shape, BF16),
        in_specs=[vmem, vmem, vmem, pl.BlockSpec(memory_space=pl.ANY), vmem],
        out_specs=vmem,
        scratch_shapes=[
            pltpu.VMEM((TILE, TILE), BF16),
            pltpu.VMEM((TILE, TILE), BF16),
            pltpu.VMEM((8, 8192), F32),
            pltpu.VMEM((16, HALF), F32),
            pltpu.VMEM((2, NZ, TILE, TILE), BF16),
            pltpu.VMEM((4, 16, 1024), BF16),
            pltpu.VMEM((2, 16, 1024), BF16),
            pltpu.VMEM((1, 8192), F32),
            pltpu.VMEM((1, TOK), jnp.int32),
            pltpu.VMEM((2, NZ, 16, HEAD), BF16),
            pltpu.VMEM((2, NZ, 16, HEAD), BF16),
            pltpu.VMEM((2, 2, TOK, TILE), BF16),
            pltpu.VMEM((NZ, 16, HALF), F32),
            pltpu.VMEM((2, 8, 2, 16, HALF), BF16),
            pltpu.VMEM((2, 8, 2, 16, HALF), BF16),
            pltpu.VMEM((ROWS, BLOCK), F32),
            pltpu.VMEM((ROWS, BLOCK), F32),
            pltpu.VMEM((16, HALF), BF16),
            pltpu.VMEM((16, HALF), BF16),
            pltpu.VMEM((2, 16, 1024), BF16),
            pltpu.VMEM((2, 16, 1024), BF16),
            dma((NZ,)),
            dma((NZ,)),
            dma((NZ,)),
            dma((6,)),
            dma((6,)),
            dma((2, NZ)),
            dma((2, NZ)),
            dma((2,)),
            dma((2,)),
            dma((2, 8, 2, NSUB)),
            dma((2, 8, 2, NSUB)),
            dma((2,)),
            dma((2,)),
        ],
        compiler_params=pltpu.CompilerParams(
            collective_id=0, has_side_effects=True, vmem_limit_bytes=40 * 1024 * 1024
        ),
    )(hidden, norm_gain, q_gain, out_weight, positions)


def solution(mesh):
    return jax.shard_map(
        per_device,
        mesh=mesh,
        in_specs=(
            P("section", "tp", None),
            P("section", None),
            P("section", None),
            P("section", "tp", None),
            P("section", None),
        ),
        out_specs=P("section", "tp", None),
        check_vma=False,
    )
```

time: 652 us -> 110 us (0.17)
  waiting for transfers between devices: 423 us -> 0 us
  Pallas kernels: 0 us -> 104 us
  blocking collectives: 60.4 us -> 0 us
  local copies, waits for them, and re-layouts: 59.1 us -> 5.83 us
  starting transfers between devices: 51.4 us -> 0 us
  other arithmetic: 24.5 us -> 0 us
  matrix products: 18.7 us -> 0 us
  between operations: 13.4 us -> 0.01 us
    all_to_all x4 -> x0, waiting for transfers between devices: 181 us -> none  [the longest x2 181 us: per_device(): lax.all_to_all(coded_split, 'tp', split_axis=1, concat_axis=0, tiled=True)]
    all_gather x3 -> x0, waiting for transfers between devices: 147 us -> none  [the longest x1 79.4 us: per_device(): state_full = lax.all_gather(hidden[0], 'tp', axis=0, tiled=True)]
    pallas_call x0 -> x1, Pallas kernels: none -> 104 us  [per_device(): pl.pallas_call(kernel, out_shape=jax.ShapeDtypeStruct(hidden.shape, BF16)...]
    ppermute x3 -> x0, waiting for transfers between devices: 95.2 us -> none  [from_behind(): return lax.ppermute(value, axis, pairs)]
    all_gather x2 -> x0, blocking collectives: 60.4 us -> none  [per_device(): lax.all_gather(rescale.astype(jnp.bfloat16), 'tp', axis=0, tiled=True)]
    all_to_all x4 -> x0, starting transfers between devices: 41.9 us -> none  [the longest x2 24.5 us: per_device(): lax.all_to_all(coded_split, 'tp', split_axis=1, concat_axis=0, tiled=True)]
    dot_general x10 -> x0, matrix products: 18.7 us -> none  [the longest x2 6.61 us: restore(): jnp.einsum('tbk,kj->tbj', pieces, table, preferred_element_type=jnp.float32)]
    mul x4 -> x0, local copies, waits for them, and re-layouts: 16.1 us -> none  [combine_terms(): coded.astype(jnp.float32).reshape(sources, count, width // BLOCK, BLOCK)]
  transfers between devices with their start and end apart: 10 -> 0, of which waited for: 7 -> 0; matrix products, arithmetic and copies ran while one was open for 7% -> 0% of each run, Pallas kernels for 0% -> 0%
where the time goes in v1:
time: 110 us
  Pallas kernels  104 us (95%)
  local copies, waits for them, and re-layouts  5.83 us (5%)
    pallas_call x1, Pallas kernels, per_device(): pl.pallas_call(kernel, out_shape=jax.ShapeDtypeStruct(hidden.shape, BF16)...  104 us
    unnamed x11, local copies, waits for them, and re-layouts  5.83 us

profile of v1, /device:TPU:1, one launch (start us, length us, event | category | flops | bytes accessed | tf_op | source)
XLA Modules:
  0.0 109.8 jit_solution(7477272712448923191)
XLA Ops:
  0.0 0.0 copy-start
  0.0 2.2 %copy-done = bf16[1,256,8192]{2,1,0:T(8,128)(2,1)S(1)} copy-done((bf16[1,256,8192]{2,1,0:T(8,128)(2,1)S(1)}, bf16[1,256,8192]{2,1,0:T(8,128)(2,1)}, u32[]{:S(2)}) %copy-start) | copy-done | bytes 4194328
  2.2 0.0 copy-start.1
  2.2 0.8 copy-done.1
  3.0 0.0 copy-start.2
  3.0 0.8 copy-done.2
  3.8 0.0 copy-start.3
  3.8 0.8 copy-done.3
  4.5 0.0 copy-start.4
  4.5 0.7 copy-done.4
  5.2 103.9 %shard_map.55 = bf16[1,4,8192]{2,1,0:T(4,128)(2,1)S(1)} custom-call(bf16[1,4,8192]{2,1,0:T(4,128)(2,1)S(1)} %copy-done.1, f32[1,8192]{1,0:T(1,128)S(1)} %copy-done.2, f32[1,8192]{1,0:T(1,128)S(1)} %copy-done.3, bf16[1,256,8192]{2,1,0:T(8,128)(2,1)S(1)} %copy-done, s32[1,128]{1,0:T(1,128)S(1)} %copy-done.4), custom_call_target="tpu_custom_call" | custom-call | tf_op jit(solution)/shard_map/pallas_call | solution.py:328
  109.2 0.6 copy.7
Async XLA Ops:
  0.0 2.2 %copy-start = (bf16[1,256,8192]{2,1,0:T(8,128)(2,1)S(1)}, bf16[1,256,8192]{2,1,0:T(8,128)(2,1)}, u32[]{:S(2)}) copy-start(bf16[1,256,8192]{2,1,0:T(8,128)(2,1)} %weight.1) | copy-start | bytes 12582916
  2.2 0.8 copy-start.1
  3.0 0.8 copy-start.2
  3.8 0.8 copy-start.3
  4.5 0.7 copy-start.4

commit v2 on v1

v2 whole, which is shorter than its diff:
```python
import jax
import jax.numpy as jnp
from jax import lax
from jax.experimental import pallas as pl
from jax.experimental.pallas import tpu as pltpu
from jax.sharding import PartitionSpec as P

MESH = pl.DeviceIdType.MESH
F32 = jnp.float32
BF16 = jnp.bfloat16
HEAD = 128
BLOCK = 128
TICKS = 2
LIMIT = 3.0
NZ = 16
TILE = 256
TOK = 128
ROWS = 8
HALF = 2048
NSUB = 4
PART = HALF // NSUB
NEAR = 4


def constants():
    rows = lax.broadcasted_iota(jnp.int32, (TILE, TILE), 0)
    cols = lax.broadcasted_iota(jnp.int32, (TILE, TILE), 1)
    same = jnp.right_shift(rows, 7) == jnp.right_shift(cols, 7)
    both = jnp.bitwise_and(rows, cols)
    for shift in (4, 2, 1):
        both = jnp.bitwise_xor(both, jnp.right_shift(both, shift)) if shift != 4 else jnp.bitwise_xor(
            jnp.bitwise_and(both, 15), jnp.bitwise_and(jnp.right_shift(both, 4), 7)
        )
    sign = (1 - 2 * jnp.bitwise_and(both, 1)).astype(F32)
    signs = jnp.where(same, sign, 0.0).astype(BF16)
    means = jnp.where(same, 1.0 / BLOCK, 0.0).astype(BF16)
    return signs, means


def swap(p, q):
    low = lax.broadcasted_iota(jnp.int32, p.shape, 0) < 4
    return (
        jnp.where(low, p, pltpu.roll(q, 4, 0)),
        jnp.where(low, pltpu.roll(p, 4, 0), q),
    )


def dot(a, b):
    return jnp.dot(a, b, preferred_element_type=F32)


def kernel(
    hidden_hbm, gain_hbm, qgain_hbm, weight, pos_hbm, out,
    hidden, gain, qgain, pos,
    signs, means, x8, st, wb, msb, mrb, gbuf, pbuf, asb, arb, cbuf, terms, sb, rb, ssb, srb, rsb, rrb, fsb, frb,
    lsem, wsem, wss, wrs, mss, mrs, ass, ars, css, crs, rss, rrs, fss, frs,
):
    sec = lax.axis_index("section")
    tp = lax.axis_index("tp")
    nsec = lax.axis_size("section")
    z = tp // 2
    k = lax.rem(tp, 2)
    sib = (sec, z * 2 + 1 - k)
    nxt = lax.rem(sec + 1, nsec)
    prv = lax.rem(sec + nsec - 1, nsec)

    def far(i):
        return lax.rem(z + i, NZ)

    def farthest(n):
        half = (n + 1) // 2
        return far(NZ // 2 + half * (1 - 2 * lax.rem(n, 2)) + NZ)

    def remote(src, dst, send, recv, device):
        return pltpu.make_async_remote_copy(
            src_ref=src, dst_ref=dst, send_sem=send, recv_sem=recv, device_id=device, device_id_type=MESH
        )

    def wcols(jj, parity):
        return pl.ds(pl.multiple_of((2 * jj + parity) * TILE, TILE), TILE)

    def wlocal(jj):
        return pltpu.make_async_copy(weight.at[0, :, wcols(jj, k)], wb.at[0, jj], wsem.at[jj])

    def wremote(jj):
        return remote(weight.at[0, :, wcols(jj, 1 - k)], wb.at[1, jj], wss.at[jj], wrs.at[jj], sib)

    def loop(n, body):
        lax.fori_loop(0, n, lambda i, c: (body(i), c)[1], 0)

    barrier = pltpu.get_barrier_semaphore()

    def greet(section, member):
        pl.semaphore_signal(barrier, inc=1, device_id=(section, member), device_id_type=MESH)

    def greet_far(n):
        greet(sec, farthest(n) * 2 + k)
        greet(prv, farthest(n) * 2 + k)

    loop(NZ - 1, greet_far)
    greet(*sib)
    greet(prv, z * 2 + k)
    greet(prv, z * 2 + 1 - k)
    greet(nxt, z * 2 + k)

    loads = [
        pltpu.make_async_copy(src, dst, lsem.at[i])
        for i, (src, dst) in enumerate(
            ((hidden_hbm, hidden), (gain_hbm, gain), (pos_hbm, pos), (qgain_hbm, qgain))
        )
    ]
    for c in loads:
        c.start()
    loop(NZ, lambda jj: wlocal(jj).start())

    sg, mn = constants()
    signs[...] = sg
    means[...] = mn

    loads[0].wait()
    x = hidden[0].astype(F32)
    x8[0:4, :] = x
    x8[4:8, :] = x
    x = x8[...]
    scale = lax.rsqrt(jnp.mean(x * x, axis=1, keepdims=True) + 1e-05)
    loads[1].wait()
    normed = x * scale * gain[...]

    def pack(v, parity):
        quarters = []
        for q in range(4):
            quarters.append(
                jnp.concatenate(
                    [v[:, (2 * jj + parity) * TILE : (2 * jj + parity + 1) * TILE] for jj in range(4 * q, 4 * q + 4)],
                    axis=1,
                )
            )
        return jnp.concatenate([swap(quarters[0], quarters[1])[0], swap(quarters[2], quarters[3])[0]], axis=0)

    even = k == 0
    for i, v in enumerate((normed, x)):
        p0, p1 = pack(v, 0), pack(v, 1)
        msb[i] = jnp.where(even, p0, p1).astype(BF16)
        msb[2 + i] = jnp.where(even, p1, p0).astype(BF16)

    loads[2].wait()
    loads[3].wait()
    pl.semaphore_wait(barrier, 2 * NZ + 2)

    packs = [remote(msb.at[2 + i], mrb.at[i], mss.at[i], mrs.at[i], sib) for i in range(2)]
    for c in packs:
        c.start()
    loop(NZ, lambda jj: wremote(jj).start())
    gains = remote(gain, gbuf, mss.at[2], mrs.at[2], (prv, z * 2 + k))
    gains.start()
    places = remote(pos, pbuf, mss.at[3], mrs.at[3], (nxt, z * 2 + k))
    places.start()

    def unpack(i):
        mine, other = msb[i].astype(F32), mrb[i].astype(F32)
        a = jnp.where(even, mine, other)
        b = jnp.where(even, other, mine)
        halves = [jnp.concatenate(swap(a[8 * h : 8 * h + 8], b[8 * h : 8 * h + 8]), axis=1) for h in range(2)]
        return jnp.concatenate(halves, axis=0)

    def a2a_copy(tick, n):
        j = farthest(n)
        return remote(
            asb.at[tick, j], arb.at[tick, z], ass.at[tick, j], ars.at[tick, z],
            (sec if tick == 0 else nxt, j * 2 + k),
        )

    def a2a_recv(tick, n):
        j = farthest(n)
        return remote(asb.at[tick, j], arb.at[tick, j], ass.at[tick, j], ars.at[tick, j], (sec, j * 2 + k))

    def spread(tick, rows):
        for jj in range(NZ):
            h, c = jj // 8, (jj % 8) * TILE
            asb[tick, jj] = jnp.concatenate(
                [rows[8 * h : 8 * h + 8, c : c + HEAD], rows[8 * h : 8 * h + 8, c + HEAD : c + 2 * HEAD]], axis=0
            ).astype(BF16)
        loop(NZ - 1 + tick, lambda n: a2a_copy(tick, n).start())
        if tick == 0:
            arb[0, z] = asb[0, z]

    packs[0].wait_recv()
    spread(0, unpack(0))
    packs[1].wait_recv()
    st[...] = unpack(1)

    def rotate(g, jj):
        if g == 0:
            wlocal(jj).wait()
        else:
            wremote(jj).wait_recv()
        wb[g, jj] = dot(wb[g, jj], signs[...]).astype(BF16)

    loop(NZ, lambda jj: rotate(0, jj))

    def attend(tick):
        rid = lax.broadcasted_iota(jnp.int32, (TOK, TOK), 0)
        cid = lax.broadcasted_iota(jnp.int32, (TOK, TOK), 1)
        row = (pos if tick == 0 else pbuf)[...].astype(F32)
        back = jnp.sum(jnp.where(rid == cid, jnp.broadcast_to(row, (TOK, TOK)), 0.0), axis=1, keepdims=True)
        seen = (cid <= rid) & (cid.astype(F32) >= rid.astype(F32) - back)
        loop(NZ - 1 + tick, lambda n: a2a_recv(tick, NZ - 2 + tick - n).wait_recv())
        v = arb[tick].astype(F32).reshape(NZ, 2, ROWS, HEAD)
        for h in range(2):
            keys = v[:, h].reshape(TOK, HEAD)
            qg = qgain[:, pl.ds(pl.multiple_of(tp * TILE + h * HEAD, HEAD), HEAD)]
            query = (keys * qg).astype(BF16)
            keys = keys.astype(BF16)
            scores = lax.dot_general(query, keys, (((1,), (1,)), ((), ())), preferred_element_type=F32) * HEAD ** (-0.5)
            scores = jnp.where(seen, scores, -1e30)
            top = jnp.max(scores, axis=1, keepdims=True)
            expo = jnp.where(seen, jnp.exp(scores - top), 0.0)
            weights = (expo / jnp.sum(expo, axis=1, keepdims=True)).astype(BF16)
            cbuf[tick, 0, :, h * HEAD : (h + 1) * HEAD] = dot(weights, keys).astype(BF16)

    def swap_context(tick):
        return remote(cbuf.at[tick, 0], cbuf.at[tick, 1], css.at[tick], crs.at[tick], sib)

    def part_terms(tick, j):
        n = PART // TILE
        for g in range(2):
            if g == 1 and j == 0:
                swap_context(tick).wait_recv()
            if g == 1 and tick == 0:
                for h in range(2):
                    for i in range(n):
                        rotate(1, h * 8 + j * n + i)
            for h in range(2):
                for i in range(n):
                    place = (slice(None), slice(h * 8, h * 8 + 8), slice(j * PART + i * TILE, j * PART + (i + 1) * TILE))
                    rotated = dot(cbuf[tick, g], wb[g, h * 8 + j * n + i])
                    bound = dot(jnp.abs(rotated).astype(BF16), means[...]) * LIMIT + LIMIT * 1e-06
                    term = jnp.clip(rotated, -bound, bound).reshape(NZ, ROWS, TILE)
                    terms[place] = term if g == 0 else terms[place] + term

    def chain(tick, dist, d, j):
        hops = dist if dist == NEAR + 1 else 1
        to = (sec, far(hops if d == 0 else NZ - hops) * 2 + k)
        cols = pl.ds(j * PART, PART)
        return remote(
            sb.at[tick, dist - 1, d, :, cols], rb.at[tick, dist - 1, d, :, cols],
            rss.at[tick, dist - 1, d, j], rrs.at[tick, dist - 1, d, j], to,
        )

    def step(tick, dist, d, j):
        if dist == 8 and j % 2 != d:
            return
        cols = slice(j * PART, (j + 1) * PART)
        v = terms[far(dist if d == 0 else NZ - dist), :, cols]
        if not (dist in (8, NEAR) or (dist == 7 and j % 2 != d)):
            chain(tick, dist + 1, d, j).wait_recv()
            v = v + rb[tick, dist, d, :, cols].astype(F32)
        sb[tick, dist - 1, d, :, cols] = v.astype(BF16)
        chain(tick, dist, d, j).start()

    def chain_sent(tick):
        def one(q):
            for j in range(NSUB):
                cols = pl.ds(j * PART, PART)
                src = sb.at[tick, q // 2, lax.rem(q, 2), :, cols]
                remote(
                    src, rb.at[tick, q // 2, lax.rem(q, 2), :, cols],
                    rss.at[tick, q // 2, lax.rem(q, 2), j], rrs.at[tick, q // 2, lax.rem(q, 2), j], sib,
                ).wait_send()

        loop(14, one)
        for j in range(NSUB):
            chain(tick, 8, j % 2, j).wait_send()

    def reduce(tick):
        for j in range(NSUB):
            part_terms(tick, j)
            for dist in (8, NEAR):
                for d in range(2):
                    step(tick, dist, d, j)
        for t in range(1, 8 - NEAR):
            for dist in (8 - t, NEAR - t):
                for j in range(NSUB):
                    for d in range(2):
                        step(tick, dist, d, j)

    def restore(tick, j):
        cols = slice(j * PART, (j + 1) * PART)
        summed = terms[z, :, cols]
        for dist in (1, NEAR + 1):
            for d in range(2):
                chain(tick, dist, d, j).wait_recv()
                summed = summed + rb[tick, dist - 1, d, :, cols].astype(F32)
        n = PART // BLOCK
        tall = jnp.concatenate([summed[:, b * BLOCK : (b + 1) * BLOCK] for b in range(n)], axis=0)
        rescale = jnp.mean(jnp.abs(tall), axis=1, keepdims=True) + 1e-06
        recoded = jnp.clip(tall / rescale, -LIMIT, LIMIT).astype(BF16)
        back = dot(recoded, signs[0:BLOCK, 0:BLOCK]) * (rescale / BLOCK)
        wide = jnp.concatenate([back[b * 16 : (b + 1) * 16] for b in range(n)], axis=1)
        return (st[:, cols] + wide).astype(BF16)

    def final(c, j):
        cols = pl.ds(j * TILE, TILE)
        return remote(
            fsb.at[c, :, cols], frb.at[k, :, cols], fss.at[c, j], frs.at[k, j], (nxt, z * 2 + c)
        )

    attend(0)
    swap_context(0).start()
    reduce(0)
    part = None
    for j in range(NSUB):
        rows = restore(0, j)
        cols = slice(j * PART, (j + 1) * PART)
        rsb[:, cols] = rows
        wide = rows.astype(F32)
        squares = jnp.sum(wide * wide, axis=1, keepdims=True)
        part = squares if part is None else part + squares
    ssb[...] = jnp.broadcast_to(part[0:8] + part[8:16], (ROWS, BLOCK))
    sums = remote(ssb, srb, mss.at[4], mrs.at[4], sib)
    sums.start()
    gains.wait_recv()
    state = rsb[...].astype(F32)
    scaled = jnp.concatenate(
        [
            state[8 * h : 8 * h + 8] * jnp.concatenate([gbuf[:, wcols(8 * h + i, k)] for i in range(8)], axis=1)
            for h in range(2)
        ],
        axis=0,
    )
    sums.wait_recv()
    scale = lax.rsqrt((ssb[:, 0:1] + srb[:, 0:1]) / (2.0 * 2 * HALF) + 1e-05)
    spread(1, scaled * jnp.concatenate([scale, scale], axis=0))
    residual = remote(rsb, rrb, mss.at[5], mrs.at[5], (nxt, z * 2 + k))
    residual.start()

    for c in packs + [gains, places, sums]:
        c.wait_send()
    loop(NZ, lambda jj: wremote(jj).wait_send())
    loop(NZ - 1, lambda n: a2a_copy(0, n).wait_send())
    swap_context(0).wait_send()
    chain_sent(0)
    places.wait_recv()

    attend(1)
    swap_context(1).start()
    reduce(1)
    residual.wait_recv()
    st[...] = rrb[...].astype(F32)
    for j in range(NSUB):
        v = restore(1, j).astype(F32)
        pair = [swap(v[8 * h : 8 * h + 8, 0:TILE], v[8 * h : 8 * h + 8, TILE:PART]) for h in range(2)]
        for c in range(2):
            fsb[c, :, j * TILE : (j + 1) * TILE] = jnp.concatenate([pair[0][c], pair[1][c]], axis=0).astype(BF16)
            final(c, j).start()

    residual.wait_send()
    loop(NZ, lambda n: a2a_copy(1, n).wait_send())
    swap_context(1).wait_send()
    chain_sent(1)
    for c in range(2):
        for j in range(NSUB):
            cols = pl.ds(j * TILE, TILE)
            remote(
                fsb.at[c, :, cols], frb.at[c, :, cols], fss.at[c, j], frs.at[c, j], (nxt, z * 2 + c)
            ).wait_recv()
    got = [frb[c].astype(F32) for c in range(2)]
    pieces = []
    for jj in range(NZ):
        h, j = jj // 8, (jj % 8) // 2
        for c in range(2):
            v = got[c][8 * h : 8 * h + 8, j * TILE : (j + 1) * TILE]
            pieces.append(pltpu.roll(v, 4, 0) if jj % 2 else v)
    out[0] = jnp.concatenate(pieces, axis=1)[0:4].astype(BF16)
    for c in range(2):
        for j in range(NSUB):
            final(c, j).wait_send()


def per_device(hidden, norm_gain, q_gain, out_weight, positions):
    vmem = pl.BlockSpec(memory_space=pltpu.VMEM)
    dma = pltpu.SemaphoreType.DMA
    return pl.pallas_call(
        kernel,
        out_shape=jax.ShapeDtypeStruct(hidden.shape, BF16),
        in_specs=[pl.BlockSpec(memory_space=pltpu.HBM)] * 5,
        out_specs=vmem,
        scratch_shapes=[
            pltpu.VMEM((1, 4, 8192), BF16),
            pltpu.VMEM((1, 8192), F32),
            pltpu.VMEM((1, 8192), F32),
            pltpu.VMEM((1, TOK), jnp.int32),
            pltpu.VMEM((TILE, TILE), BF16),
            pltpu.VMEM((TILE, TILE), BF16),
            pltpu.VMEM((8, 8192), F32),
            pltpu.VMEM((16, HALF), F32),
            pltpu.VMEM((2, NZ, TILE, TILE), BF16),
            pltpu.VMEM((4, 16, 1024), BF16),
            pltpu.VMEM((2, 16, 1024), BF16),
            pltpu.VMEM((1, 8192), F32),
            pltpu.VMEM((1, TOK), jnp.int32),
            pltpu.VMEM((2, NZ, 16, HEAD), BF16),
            pltpu.VMEM((2, NZ, 16, HEAD), BF16),
            pltpu.VMEM((2, 2, TOK, TILE), BF16),
            pltpu.VMEM((NZ, 16, HALF), F32),
            pltpu.VMEM((2, 8, 2, 16, HALF), BF16),
            pltpu.VMEM((2, 8, 2, 16, HALF), BF16),
            pltpu.VMEM((ROWS, BLOCK), F32),
            pltpu.VMEM((ROWS, BLOCK), F32),
            pltpu.VMEM((16, HALF), BF16),
            pltpu.VMEM((16, HALF), BF16),
            pltpu.VMEM((2, 16, 1024), BF16),
            pltpu.VMEM((2, 16, 1024), BF16),
            dma((4,)),
            dma((NZ,)),
            dma((NZ,)),
            dma((NZ,)),
            dma((6,)),
            dma((6,)),
            dma((2, NZ)),
            dma((2, NZ)),
            dma((2,)),
            dma((2,)),
            dma((2, 8, 2, NSUB)),
            dma((2, 8, 2, NSUB)),
            dma((2, NSUB)),
            dma((2, NSUB)),
        ],
        compiler_params=pltpu.CompilerParams(
            collective_id=0, has_side_effects=True, vmem_limit_bytes=60 * 1024 * 1024
        ),
    )(hidden, norm_gain, q_gain, out_weight, positions)


def solution(mesh):
    return jax.shard_map(
        per_device,
        mesh=mesh,
        in_specs=(
            P("section", "tp", None),
            P("section", None),
            P("section", None),
            P("section", "tp", None),
            P("section", None),
        ),
        out_specs=P("section", "tp", None),
        check_vma=False,
    )
```

time: 110 us -> 94.2 us (0.86)
  Pallas kernels: 104 us -> 92.5 us
  local copies, waits for them, and re-layouts: 5.83 us -> 1.49 us
    pallas_call x1, Pallas kernels: 104 us -> 92.5 us  [per_device(): pl.pallas_call(kernel, out_shape=jax.ShapeDtypeStruct(hidden.shape, BF16)...]
    unnamed x11 -> x1, local copies, waits for them, and re-layouts: 5.83 us -> 1.49 us
where the time goes in v2:
time: 94.2 us; the launch traced here: 94 us
  Pallas kernels  92.5 us (98%)
  local copies, waits for them, and re-layouts  1.49 us (2%)
    pallas_call x1, Pallas kernels, per_device(): pl.pallas_call(kernel, out_shape=jax.ShapeDtypeStruct(hidden.shape, BF16)...  92.5 us

profile of v2, /device:TPU:1, one launch (start us, length us, event | category | flops | bytes accessed | tf_op | source)
XLA Modules:
  0.0 94.0 jit_solution(8753469796631487501)
XLA Ops:
  0.0 92.5 %shard_map.55 = bf16[1,4,8192]{2,1,0:T(4,128)(2,1)} custom-call(bf16[1,4,8192]{2,1,0:T(4,128)(2,1)} %hidden_hbm.1, f32[1,8192]{1,0:T(1,128)} %gain_hbm.1, f32[1,8192]{1,0:T(1,128)} %qgain_hbm.1, bf16[1,256,8192]{2,1,0:T(8,128)(2,1)} %weight.1, s32[1,128]{1,0:T(1,128)} %pos_hbm.1), custom_call_target="tpu_custom_call" | custom-call | tf_op jit(solution)/shard_map/pallas_call | solution.py:383
  92.5 1.5 %copy.7 = bf16[1,4,8192]{2,1,0:T(4,128)(2,1)} copy(bf16[1,4,8192]{2,1,0:T(4,128)(2,1)} %shard_map.55) | data formatting | bytes 131072

commit v3 on v2

--- a/solution.py
+++ b/solution.py
@@ -19,6 +19,7 @@
 HALF = 2048
 NSUB = 4
 PART = HALF // NSUB
+EARLY = 6
 NEAR = 4
 
 
@@ -52,8 +53,8 @@
 def kernel(
     hidden_hbm, gain_hbm, qgain_hbm, weight, pos_hbm, out,
     hidden, gain, qgain, pos,
-    signs, means, x8, st, wb, msb, mrb, gbuf, pbuf, asb, arb, cbuf, terms, sb, rb, ssb, srb, rsb, rrb, fsb, frb,
-    lsem, wsem, wss, wrs, mss, mrs, ass, ars, css, crs, rss, rrs, fss, frs,
+    signs, means, x8, st, wb, msb, mrb, gbuf, pbuf, asb, arb, cbuf, terms, sb, rb, ssb, srb, rsb, rrb, fsb, frb, rly,
+    lsem, wsem, wss, wrs, mss, mrs, ass, ars, css, crs, rss, rrs, fss, frs, pss, rlr, sqs, sqr,
 ):
     sec = lax.axis_index("section")
     tp = lax.axis_index("tp")
@@ -93,15 +94,24 @@
     def greet(section, member):
         pl.semaphore_signal(barrier, inc=1, device_id=(section, member), device_id_type=MESH)
 
-    def greet_far(n):
-        greet(sec, farthest(n) * 2 + k)
-        greet(prv, farthest(n) * 2 + k)
-
-    loop(NZ - 1, greet_far)
+    order = [8, 7, 9, 6, 10, 5, 11, 4, 12, 3, 13, 2, 14, 1, 15]
+    relayed = [i for i in order if 4 < i < 12]
+
+    def by_relay(source, i):
+        return jnp.logical_and(source < EARLY, lax.rem(source + i, NZ) >= EARLY)
+
+    for i in order:
+        if i in relayed:
+            pl.when(jnp.logical_not(by_relay(far(NZ - i), i)))(lambda i=i: greet(sec, far(NZ - i) * 2 + k))
+        else:
+            greet(sec, far(NZ - i) * 2 + k)
     greet(*sib)
     greet(prv, z * 2 + k)
     greet(prv, z * 2 + 1 - k)
     greet(nxt, z * 2 + k)
+    direct = NZ - 1 + 4
+    for i in relayed:
+        direct = direct - by_relay(z, i).astype(jnp.int32)
 
     loads = [
         pltpu.make_async_copy(src, dst, lsem.at[i])
@@ -112,10 +122,6 @@
     for c in loads:
         c.start()
     loop(NZ, lambda jj: wlocal(jj).start())
-
-    sg, mn = constants()
-    signs[...] = sg
-    means[...] = mn
 
     loads[0].wait()
     x = hidden[0].astype(F32)
@@ -138,23 +144,19 @@
         return jnp.concatenate([swap(quarters[0], quarters[1])[0], swap(quarters[2], quarters[3])[0]], axis=0)
 
     even = k == 0
-    for i, v in enumerate((normed, x)):
+
+    def pack_both(i, v):
         p0, p1 = pack(v, 0), pack(v, 1)
         msb[i] = jnp.where(even, p0, p1).astype(BF16)
         msb[2 + i] = jnp.where(even, p1, p0).astype(BF16)
 
-    loads[2].wait()
-    loads[3].wait()
-    pl.semaphore_wait(barrier, 2 * NZ + 2)
-
+    pack_both(0, normed)
+    pl.semaphore_wait(barrier, direct)
     packs = [remote(msb.at[2 + i], mrb.at[i], mss.at[i], mrs.at[i], sib) for i in range(2)]
-    for c in packs:
-        c.start()
-    loop(NZ, lambda jj: wremote(jj).start())
+    packs[0].start()
+    pack_both(1, x)
     gains = remote(gain, gbuf, mss.at[2], mrs.at[2], (prv, z * 2 + k))
-    gains.start()
     places = remote(pos, pbuf, mss.at[3], mrs.at[3], (nxt, z * 2 + k))
-    places.start()
 
     def unpack(i):
         mine, other = msb[i].astype(F32), mrb[i].astype(F32)
@@ -163,8 +165,7 @@
         halves = [jnp.concatenate(swap(a[8 * h : 8 * h + 8], b[8 * h : 8 * h + 8]), axis=1) for h in range(2)]
         return jnp.concatenate(halves, axis=0)
 
-    def a2a_copy(tick, n):
-        j = farthest(n)
+    def a2a_copy(tick, j):
         return remote(
             asb.at[tick, j], arb.at[tick, z], ass.at[tick, j], ars.at[tick, z],
             (sec if tick == 0 else nxt, j * 2 + k),
@@ -174,40 +175,94 @@
         j = farthest(n)
         return remote(asb.at[tick, j], arb.at[tick, j], ass.at[tick, j], ars.at[tick, j], (sec, j * 2 + k))
 
-    def spread(tick, rows):
-        for jj in range(NZ):
-            h, c = jj // 8, (jj % 8) * TILE
-            asb[tick, jj] = jnp.concatenate(
-                [rows[8 * h : 8 * h + 8, c : c + HEAD], rows[8 * h : 8 * h + 8, c + HEAD : c + 2 * HEAD]], axis=0
-            ).astype(BF16)
-        loop(NZ - 1 + tick, lambda n: a2a_copy(tick, n).start())
-        if tick == 0:
-            arb[0, z] = asb[0, z]
+    def message(tick, jj, v):
+        asb[tick, jj] = jnp.concatenate([v[:, 0:HEAD], v[:, HEAD:TILE]], axis=0).astype(BF16)
+
+    def square_copy(n, c):
+        j = farthest(n)
+        return remote(ssb, srb.at[tp], sqs.at[j * 2 + c], sqr.at[tp], (nxt, j * 2 + c))
+
+    def pass_copy(i):
+        origin = far(NZ - 4 if i <= 8 else 4)
+        to = (sec, lax.rem(origin + i, NZ) * 2 + k)
+        return remote(rly.at[i - 5], arb.at[0, origin], pss.at[i - 5], ars.at[0, origin], to)
+
+    def relay_copy(i):
+        to = (sec, far(4 if i <= 8 else NZ - 4) * 2 + k)
+        return remote(asb.at[0, far(i)], rly.at[i - 5], ass.at[0, far(i)], rlr.at[i - 5], to)
+
+    def direct_copy(i):
+        return remote(asb.at[0, far(i)], arb.at[0, z], ass.at[0, far(i)], ars.at[0, z], (sec, far(i) * 2 + k))
+
+    def passes(i):
+        return by_relay(far(NZ - 4 if i <= 8 else 4), i)
+
+    def first_sends():
+        for i in order:
+            if i in relayed:
+                pl.when(by_relay(z, i))(lambda i=i: relay_copy(i).start())
+                pl.when(jnp.logical_not(by_relay(z, i)))(lambda i=i: direct_copy(i).start())
+            else:
+                direct_copy(i).start()
+        arb[0, z] = asb[0, z]
+
+        packs[1].start()
+        loop(NZ, lambda jj: wremote(jj).start())
+        loads[2].wait()
+        loads[3].wait()
+        gains.start()
+        places.start()
+
+        def hand_on(i):
+            relay_copy(i).wait_recv()
+            pass_copy(i).start()
+
+        for i in relayed:
+            pl.when(passes(i))(lambda i=i: hand_on(i))
 
     packs[0].wait_recv()
-    spread(0, unpack(0))
+    rows = unpack(0)
+    for jj in range(NZ):
+        h, c = jj // 8, (jj % 8) * TILE
+        message(0, jj, rows[8 * h : 8 * h + 8, c : c + TILE])
+    first_sends()
     packs[1].wait_recv()
     st[...] = unpack(1)
 
-    def rotate(g, jj):
-        if g == 0:
-            wlocal(jj).wait()
-        else:
-            wremote(jj).wait_recv()
-        wb[g, jj] = dot(wb[g, jj], signs[...]).astype(BF16)
-
-    loop(NZ, lambda jj: rotate(0, jj))
+    def rotate(g, quarter):
+        places = [quarter * 4 + i for i in range(4)]
+        for jj in places:
+            if g == 0:
+                wlocal(jj).wait()
+            else:
+                wremote(jj).wait_recv()
+        for jj in places:
+            wb[g, jj] = dot(wb[g, jj], signs[...]).astype(BF16)
+
+    sg, mn = constants()
+    signs[...] = sg
+    means[...] = mn
+    loop(4, lambda quarter: rotate(0, quarter))
+    loop(4, lambda quarter: rotate(1, quarter))
 
     def attend(tick):
         rid = lax.broadcasted_iota(jnp.int32, (TOK, TOK), 0)
         cid = lax.broadcasted_iota(jnp.int32, (TOK, TOK), 1)
-        row = (pos if tick == 0 else pbuf)[...].astype(F32)
-        back = jnp.sum(jnp.where(rid == cid, jnp.broadcast_to(row, (TOK, TOK)), 0.0), axis=1, keepdims=True)
+
+        def upright(row):
+            return jnp.sum(jnp.where(rid == cid, jnp.broadcast_to(row, (TOK, TOK)), 0.0), axis=1, keepdims=True)
+
+        back = upright((pos if tick == 0 else pbuf)[...].astype(F32))
         seen = (cid <= rid) & (cid.astype(F32) >= rid.astype(F32) - back)
         loop(NZ - 1 + tick, lambda n: a2a_recv(tick, NZ - 2 + tick - n).wait_recv())
         v = arb[tick].astype(F32).reshape(NZ, 2, ROWS, HEAD)
+        if tick:
+            loop(2 * NZ, lambda m: remote(ssb, srb.at[m], sqs.at[m], sqr.at[m], sib).wait_recv())
+            scale = upright(lax.rsqrt(jnp.sum(srb[...], axis=0) / (4.0 * HALF) + 1e-05))
         for h in range(2):
             keys = v[:, h].reshape(TOK, HEAD)
+            if tick:
+                keys = (keys * scale).astype(BF16).astype(F32)
             qg = qgain[:, pl.ds(pl.multiple_of(tp * TILE + h * HEAD, HEAD), HEAD)]
             query = (keys * qg).astype(BF16)
             keys = keys.astype(BF16)
@@ -226,10 +281,6 @@
         for g in range(2):
             if g == 1 and j == 0:
                 swap_context(tick).wait_recv()
-            if g == 1 and tick == 0:
-                for h in range(2):
-                    for i in range(n):
-                        rotate(1, h * 8 + j * n + i)
             for h in range(2):
                 for i in range(n):
                     place = (slice(None), slice(h * 8, h * 8 + 8), slice(j * PART + i * TILE, j * PART + (i + 1) * TILE))
@@ -284,20 +335,24 @@
                     for d in range(2):
                         step(tick, dist, d, j)
 
-    def restore(tick, j):
-        cols = slice(j * PART, (j + 1) * PART)
-        summed = terms[z, :, cols]
-        for dist in (1, NEAR + 1):
-            for d in range(2):
-                chain(tick, dist, d, j).wait_recv()
-                summed = summed + rb[tick, dist - 1, d, :, cols].astype(F32)
-        n = PART // BLOCK
+    def restore(tick):
+        sums = []
+        for j in range(NSUB):
+            cols = slice(j * PART, (j + 1) * PART)
+            summed = terms[z, :, cols]
+            for dist in (1, NEAR + 1):
+                for d in range(2):
+                    chain(tick, dist, d, j).wait_recv()
+                    summed = summed + rb[tick, dist - 1, d, :, cols].astype(F32)
+            sums.append(summed)
+        summed = jnp.concatenate(sums, axis=1)
+        n = HALF // BLOCK
         tall = jnp.concatenate([summed[:, b * BLOCK : (b + 1) * BLOCK] for b in range(n)], axis=0)
         rescale = jnp.mean(jnp.abs(tall), axis=1, keepdims=True) + 1e-06
         recoded = jnp.clip(tall / rescale, -LIMIT, LIMIT).astype(BF16)
         back = dot(recoded, signs[0:BLOCK, 0:BLOCK]) * (rescale / BLOCK)
         wide = jnp.concatenate([back[b * 16 : (b + 1) * 16] for b in range(n)], axis=1)
-        return (st[:, cols] + wide).astype(BF16)
+        return (st[...] + wide).astype(BF16)
 
     def final(c, j):
         cols = pl.ds(j * TILE, TILE)
@@ -308,36 +363,28 @@
     attend(0)
     swap_context(0).start()
     reduce(0)
-    part = None
-    for j in range(NSUB):
-        rows = restore(0, j)
-        cols = slice(j * PART, (j + 1) * PART)
-        rsb[:, cols] = rows
-        wide = rows.astype(F32)
-        squares = jnp.sum(wide * wide, axis=1, keepdims=True)
-        part = squares if part is None else part + squares
-    ssb[...] = jnp.broadcast_to(part[0:8] + part[8:16], (ROWS, BLOCK))
-    sums = remote(ssb, srb, mss.at[4], mrs.at[4], sib)
-    sums.start()
     gains.wait_recv()
-    state = rsb[...].astype(F32)
-    scaled = jnp.concatenate(
-        [
-            state[8 * h : 8 * h + 8] * jnp.concatenate([gbuf[:, wcols(8 * h + i, k)] for i in range(8)], axis=1)
-            for h in range(2)
-        ],
-        axis=0,
-    )
-    sums.wait_recv()
-    scale = lax.rsqrt((ssb[:, 0:1] + srb[:, 0:1]) / (2.0 * 2 * HALF) + 1e-05)
-    spread(1, scaled * jnp.concatenate([scale, scale], axis=0))
-    residual = remote(rsb, rrb, mss.at[5], mrs.at[5], (nxt, z * 2 + k))
+    rows = restore(0)
+    rsb[...] = rows
+    wide = rows.astype(F32)
+    squares = jnp.sum(wide * wide, axis=1, keepdims=True)
+    token = lax.broadcasted_iota(jnp.int32, (ROWS, TOK), 0) + z * ROWS
+    lane = lax.broadcasted_iota(jnp.int32, (ROWS, TOK), 1)
+    ssb[...] = jnp.sum(jnp.where(token == lane, squares[0:8] + squares[8:16], 0.0), axis=0, keepdims=True)
+    loop(NZ, lambda n: (square_copy(n, 0).start(), square_copy(n, 1).start()))
+    for jj in range(NZ):
+        h, c = jj // 8, (jj % 8) * TILE
+        message(1, jj, wide[8 * h : 8 * h + 8, c : c + TILE] * gbuf[:, wcols(jj, k)])
+    loop(NZ, lambda n: a2a_copy(1, farthest(n)).start())
+    residual = remote(rsb, rrb, mss.at[4], mrs.at[4], (nxt, z * 2 + k))
     residual.start()
 
-    for c in packs + [gains, places, sums]:
+    for c in packs + [gains, places]:
         c.wait_send()
     loop(NZ, lambda jj: wremote(jj).wait_send())
-    loop(NZ - 1, lambda n: a2a_copy(0, n).wait_send())
+    loop(NZ - 1, lambda n: a2a_copy(0, farthest(n)).wait_send())
+    for i in relayed:
+        pl.when(passes(i))(lambda i=i: pass_copy(i).wait_send())
     swap_context(0).wait_send()
     chain_sent(0)
     places.wait_recv()
@@ -347,15 +394,18 @@
     reduce(1)
     residual.wait_recv()
     st[...] = rrb[...].astype(F32)
+    rows = restore(1).astype(F32)
     for j in range(NSUB):
-        v = restore(1, j).astype(F32)
+        v = rows[:, j * PART : (j + 1) * PART]
         pair = [swap(v[8 * h : 8 * h + 8, 0:TILE], v[8 * h : 8 * h + 8, TILE:PART]) for h in range(2)]
         for c in range(2):
             fsb[c, :, j * TILE : (j + 1) * TILE] = jnp.concatenate([pair[0][c], pair[1][c]], axis=0).astype(BF16)
+    for j in range(NSUB):
+        for c in range(2):
             final(c, j).start()
 
     residual.wait_send()
-    loop(NZ, lambda n: a2a_copy(1, n).wait_send())
+    loop(NZ, lambda n: (a2a_copy(1, n).wait_send(), square_copy(n, 0).wait_send(), square_copy(n, 1).wait_send()))
     swap_context(1).wait_send()
     chain_sent(1)
     for c in range(2):
@@ -405,18 +455,19 @@
             pltpu.VMEM((NZ, 16, HALF), F32),
             pltpu.VMEM((2, 8, 2, 16, HALF), BF16),
             pltpu.VMEM((2, 8, 2, 16, HALF), BF16),
-            pltpu.VMEM((ROWS, BLOCK), F32),
-            pltpu.VMEM((ROWS, BLOCK), F32),
+            pltpu.VMEM((1, TOK), F32),
+            pltpu.VMEM((2 * NZ, 1, TOK), F32),
             pltpu.VMEM((16, HALF), BF16),
             pltpu.VMEM((16, HALF), BF16),
             pltpu.VMEM((2, 16, 1024), BF16),
             pltpu.VMEM((2, 16, 1024), BF16),
+            pltpu.VMEM((7, 16, HEAD), BF16),
             dma((4,)),
             dma((NZ,)),
             dma((NZ,)),
             dma((NZ,)),
-            dma((6,)),
-            dma((6,)),
+            dma((5,)),
+            dma((5,)),
             dma((2, NZ)),
             dma((2, NZ)),
             dma((2,)),
@@ -425,6 +476,10 @@
             dma((2, 8, 2, NSUB)),
             dma((2, NSUB)),
             dma((2, NSUB)),
+            dma((7,)),
+            dma((7,)),
+            dma((2 * NZ,)),
+            dma((2 * NZ,)),
         ],
         compiler_params=pltpu.CompilerParams(
             collective_id=0, has_side_effects=True, vmem_limit_bytes=60 * 1024 * 1024

time: 94.2 us -> 91.4 us (0.970)
  Pallas kernels: 92.5 us -> 89.7 us
    pallas_call x1, Pallas kernels: 92.5 us -> 89.7 us  [per_device(): pl.pallas_call(kernel, out_shape=jax.ShapeDtypeStruct(hidden.shape, BF16)...]
where the time goes in v3:
time: 91.4 us; the launch traced here: 91.2 us
  Pallas kernels  89.7 us (98%)
  local copies, waits for them, and re-layouts  1.49 us (2%)
    pallas_call x1, Pallas kernels, per_device(): pl.pallas_call(kernel, out_shape=jax.ShapeDtypeStruct(hidden.shape, BF16)...  89.7 us

profile of v3, /device:TPU:1, one launch (start us, length us, event | category | flops | bytes accessed | tf_op | source)
XLA Modules:
  0.0 91.2 jit_solution(2889453551047502054)
XLA Ops:
  0.0 89.7 %shard_map.55 = bf16[1,4,8192]{2,1,0:T(4,128)(2,1)} custom-call(bf16[1,4,8192]{2,1,0:T(4,128)(2,1)} %hidden_hbm.1, f32[1,8192]{1,0:T(1,128)} %gain_hbm.1, f32[1,8192]{1,0:T(1,128)} %qgain_hbm.1, bf16[1,256,8192]{2,1,0:T(8,128)(2,1)} %weight.1, s32[1,128]{1,0:T(1,128)} %pos_hbm.1), custom_call_target="tpu_custom_call" | custom-call | tf_op jit(solution)/shard_map/pallas_call | solution.py:433
  89.8 1.5 %copy.7 = bf16[1,4,8192]{2,1,0:T(4,128)(2,1)} copy(bf16[1,4,8192]{2,1,0:T(4,128)(2,1)} %shard_map.55) | data formatting | bytes 131072

commit v4 on v3

--- a/solution.py
+++ b/solution.py
@@ -19,6 +19,7 @@
 HALF = 2048
 NSUB = 4
 PART = HALF // NSUB
+AHEAD = 3
 EARLY = 6
 NEAR = 4
 
@@ -81,13 +82,22 @@
         return pl.ds(pl.multiple_of((2 * jj + parity) * TILE, TILE), TILE)
 
     def wlocal(jj):
-        return pltpu.make_async_copy(weight.at[0, :, wcols(jj, k)], wb.at[0, jj], wsem.at[jj])
+        return pltpu.make_async_copy(weight.at[0, :, wcols(jj, k)], wb.at[0, jj], wsem.at[jj // 4])
 
     def wremote(jj):
-        return remote(weight.at[0, :, wcols(jj, 1 - k)], wb.at[1, jj], wss.at[jj], wrs.at[jj], sib)
+        return remote(weight.at[0, :, wcols(jj, 1 - k)], wb.at[1, jj], wss.at[0], wrs.at[jj // 4], sib)
 
     def loop(n, body):
         lax.fori_loop(0, n, lambda i, c: (body(i), c)[1], 0)
+
+    loads = [
+        pltpu.make_async_copy(src, dst, lsem.at[i])
+        for i, (src, dst) in enumerate(
+            ((hidden_hbm, hidden), (gain_hbm, gain), (pos_hbm, pos), (qgain_hbm, qgain))
+        )
+    ]
+    for c in loads[:2]:
+        c.start()
 
     barrier = pltpu.get_barrier_semaphore()
 
@@ -113,13 +123,7 @@
     for i in relayed:
         direct = direct - by_relay(z, i).astype(jnp.int32)
 
-    loads = [
-        pltpu.make_async_copy(src, dst, lsem.at[i])
-        for i, (src, dst) in enumerate(
-            ((hidden_hbm, hidden), (gain_hbm, gain), (pos_hbm, pos), (qgain_hbm, qgain))
-        )
-    ]
-    for c in loads:
+    for c in loads[2:]:
         c.start()
     loop(NZ, lambda jj: wlocal(jj).start())
 
@@ -167,32 +171,31 @@
 
     def a2a_copy(tick, j):
         return remote(
-            asb.at[tick, j], arb.at[tick, z], ass.at[tick, j], ars.at[tick, z],
-            (sec if tick == 0 else nxt, j * 2 + k),
+            asb.at[tick, j], arb.at[tick, z], ass.at[tick], ars.at[tick], (sec if tick == 0 else nxt, j * 2 + k)
         )
 
-    def a2a_recv(tick, n):
-        j = farthest(n)
-        return remote(asb.at[tick, j], arb.at[tick, j], ass.at[tick, j], ars.at[tick, j], (sec, j * 2 + k))
+    def a2a_all(tick):
+        some = pl.ds(0, NZ - 1 + tick)
+        return remote(asb.at[tick, some], arb.at[tick, some], ass.at[tick], ars.at[tick], sib)
 
     def message(tick, jj, v):
         asb[tick, jj] = jnp.concatenate([v[:, 0:HEAD], v[:, HEAD:TILE]], axis=0).astype(BF16)
 
     def square_copy(n, c):
         j = farthest(n)
-        return remote(ssb, srb.at[tp], sqs.at[j * 2 + c], sqr.at[tp], (nxt, j * 2 + c))
+        return remote(ssb.at[j * 2 + c], srb.at[tp], sqs.at[0], sqr.at[0], (nxt, j * 2 + c))
+
+    def squares_all():
+        return remote(ssb, srb, sqs.at[0], sqr.at[0], sib)
 
     def pass_copy(i):
         origin = far(NZ - 4 if i <= 8 else 4)
         to = (sec, lax.rem(origin + i, NZ) * 2 + k)
-        return remote(rly.at[i - 5], arb.at[0, origin], pss.at[i - 5], ars.at[0, origin], to)
+        return remote(rly.at[i - 5], arb.at[0, origin], pss.at[i - 5], ars.at[0], to)
 
     def relay_copy(i):
         to = (sec, far(4 if i <= 8 else NZ - 4) * 2 + k)
-        return remote(asb.at[0, far(i)], rly.at[i - 5], ass.at[0, far(i)], rlr.at[i - 5], to)
-
-    def direct_copy(i):
-        return remote(asb.at[0, far(i)], arb.at[0, z], ass.at[0, far(i)], ars.at[0, z], (sec, far(i) * 2 + k))
+        return remote(asb.at[0, far(i)], rly.at[i - 5], ass.at[0], rlr.at[i - 5], to)
 
     def passes(i):
         return by_relay(far(NZ - 4 if i <= 8 else 4), i)
@@ -201,9 +204,9 @@
         for i in order:
             if i in relayed:
                 pl.when(by_relay(z, i))(lambda i=i: relay_copy(i).start())
-                pl.when(jnp.logical_not(by_relay(z, i)))(lambda i=i: direct_copy(i).start())
+                pl.when(jnp.logical_not(by_relay(z, i)))(lambda i=i: a2a_copy(0, far(i)).start())
             else:
-                direct_copy(i).start()
+                a2a_copy(0, far(i)).start()
         arb[0, z] = asb[0, z]
 
         packs[1].start()
@@ -231,11 +234,11 @@
 
     def rotate(g, quarter):
         places = [quarter * 4 + i for i in range(4)]
-        for jj in places:
-            if g == 0:
-                wlocal(jj).wait()
-            else:
-                wremote(jj).wait_recv()
+        four = wb.at[g, pl.ds(quarter * 4, 4)]
+        if g == 0:
+            pltpu.make_async_copy(four, four, wsem.at[quarter]).wait()
+        else:
+            remote(four, four, wss.at[0], wrs.at[quarter], sib).wait_recv()
         for jj in places:
             wb[g, jj] = dot(wb[g, jj], signs[...]).astype(BF16)
 
@@ -254,10 +257,10 @@
 
         back = upright((pos if tick == 0 else pbuf)[...].astype(F32))
         seen = (cid <= rid) & (cid.astype(F32) >= rid.astype(F32) - back)
-        loop(NZ - 1 + tick, lambda n: a2a_recv(tick, NZ - 2 + tick - n).wait_recv())
+        a2a_all(tick).wait_recv()
         v = arb[tick].astype(F32).reshape(NZ, 2, ROWS, HEAD)
         if tick:
-            loop(2 * NZ, lambda m: remote(ssb, srb.at[m], sqs.at[m], sqr.at[m], sib).wait_recv())
+            squares_all().wait_recv()
             scale = upright(lax.rsqrt(jnp.sum(srb[...], axis=0) / (4.0 * HALF) + 1e-05))
         for h in range(2):
             keys = v[:, h].reshape(TOK, HEAD)
@@ -276,18 +279,15 @@
     def swap_context(tick):
         return remote(cbuf.at[tick, 0], cbuf.at[tick, 1], css.at[tick], crs.at[tick], sib)
 
-    def part_terms(tick, j):
+    def part_terms(tick, g, j):
         n = PART // TILE
-        for g in range(2):
-            if g == 1 and j == 0:
-                swap_context(tick).wait_recv()
-            for h in range(2):
-                for i in range(n):
-                    place = (slice(None), slice(h * 8, h * 8 + 8), slice(j * PART + i * TILE, j * PART + (i + 1) * TILE))
-                    rotated = dot(cbuf[tick, g], wb[g, h * 8 + j * n + i])
-                    bound = dot(jnp.abs(rotated).astype(BF16), means[...]) * LIMIT + LIMIT * 1e-06
-                    term = jnp.clip(rotated, -bound, bound).reshape(NZ, ROWS, TILE)
-                    terms[place] = term if g == 0 else terms[place] + term
+        for h in range(2):
+            for i in range(n):
+                place = (slice(None), slice(h * 8, h * 8 + 8), slice(j * PART + i * TILE, j * PART + (i + 1) * TILE))
+                rotated = dot(cbuf[tick, g], wb[g, h * 8 + j * n + i])
+                bound = dot(jnp.abs(rotated).astype(BF16), means[...]) * LIMIT + LIMIT * 1e-06
+                term = jnp.clip(rotated, -bound, bound).reshape(NZ, ROWS, TILE)
+                terms[place] = term if g == 0 else terms[place] + term
 
     def chain(tick, dist, d, j):
         hops = dist if dist == NEAR + 1 else 1
@@ -295,8 +295,15 @@
         cols = pl.ds(j * PART, PART)
         return remote(
             sb.at[tick, dist - 1, d, :, cols], rb.at[tick, dist - 1, d, :, cols],
-            rss.at[tick, dist - 1, d, j], rrs.at[tick, dist - 1, d, j], to,
+            rss.at[tick, dist // 8], rrs.at[tick, dist - 1, d, j // 2], to,
         )
+
+    def arrive(tick, dist, d, j):
+        if dist == 8:
+            chain(tick, 8, d, j).wait_recv()
+        elif j % 2 == 0:
+            both = rb.at[tick, dist - 1, d, :, pl.ds(j * PART, 2 * PART)]
+            remote(both, both, rss.at[tick, 0], rrs.at[tick, dist - 1, d, j // 2], sib).wait_recv()
 
     def step(tick, dist, d, j):
         if dist == 8 and j % 2 != d:
@@ -304,28 +311,24 @@
         cols = slice(j * PART, (j + 1) * PART)
         v = terms[far(dist if d == 0 else NZ - dist), :, cols]
         if not (dist in (8, NEAR) or (dist == 7 and j % 2 != d)):
-            chain(tick, dist + 1, d, j).wait_recv()
+            arrive(tick, dist + 1, d, j)
             v = v + rb[tick, dist, d, :, cols].astype(F32)
         sb[tick, dist - 1, d, :, cols] = v.astype(BF16)
         chain(tick, dist, d, j).start()
 
     def chain_sent(tick):
-        def one(q):
-            for j in range(NSUB):
-                cols = pl.ds(j * PART, PART)
-                src = sb.at[tick, q // 2, lax.rem(q, 2), :, cols]
-                remote(
-                    src, rb.at[tick, q // 2, lax.rem(q, 2), :, cols],
-                    rss.at[tick, q // 2, lax.rem(q, 2), j], rrs.at[tick, q // 2, lax.rem(q, 2), j], sib,
-                ).wait_send()
-
-        loop(14, one)
+        most, rest = sb.at[tick, pl.ds(0, 7)], sb.at[tick, 7, 0]
+        remote(most, most, rss.at[tick, 0], rrs.at[tick, 0, 0, 0], sib).wait_send()
+        remote(rest, rest, rss.at[tick, 1], rrs.at[tick, 0, 0, 0], sib).wait_send()
+
+    def reduce(tick):
+        for j in range(AHEAD):
+            part_terms(tick, 0, j)
+        swap_context(tick).wait_recv()
         for j in range(NSUB):
-            chain(tick, 8, j % 2, j).wait_send()
-
-    def reduce(tick):
-        for j in range(NSUB):
-            part_terms(tick, j)
+            if j >= AHEAD:
+                part_terms(tick, 0, j)
+            part_terms(tick, 1, j)
             for dist in (8, NEAR):
                 for d in range(2):
                     step(tick, dist, d, j)
@@ -342,7 +345,7 @@
             summed = terms[z, :, cols]
             for dist in (1, NEAR + 1):
                 for d in range(2):
-                    chain(tick, dist, d, j).wait_recv()
+                    arrive(tick, dist, d, j)
                     summed = summed + rb[tick, dist - 1, d, :, cols].astype(F32)
             sums.append(summed)
         summed = jnp.concatenate(sums, axis=1)
@@ -356,9 +359,9 @@
 
     def final(c, j):
         cols = pl.ds(j * TILE, TILE)
-        return remote(
-            fsb.at[c, :, cols], frb.at[k, :, cols], fss.at[c, j], frs.at[k, j], (nxt, z * 2 + c)
-        )
+        return remote(fsb.at[c, :, cols], frb.at[k, :, cols], fss.at[0], frs.at[0], (nxt, z * 2 + c))
+
+    finals = remote(fsb, frb, fss.at[0], frs.at[0], sib)
 
     attend(0)
     swap_context(0).start()
@@ -370,7 +373,9 @@
     squares = jnp.sum(wide * wide, axis=1, keepdims=True)
     token = lax.broadcasted_iota(jnp.int32, (ROWS, TOK), 0) + z * ROWS
     lane = lax.broadcasted_iota(jnp.int32, (ROWS, TOK), 1)
-    ssb[...] = jnp.sum(jnp.where(token == lane, squares[0:8] + squares[8:16], 0.0), axis=0, keepdims=True)
+    squares = jnp.sum(jnp.where(token == lane, squares[0:8] + squares[8:16], 0.0), axis=0, keepdims=True)
+    for m in range(2 * NZ):
+        ssb[m] = squares
     loop(NZ, lambda n: (square_copy(n, 0).start(), square_copy(n, 1).start()))
     for jj in range(NZ):
         h, c = jj // 8, (jj % 8) * TILE
@@ -381,8 +386,8 @@
 
     for c in packs + [gains, places]:
         c.wait_send()
-    loop(NZ, lambda jj: wremote(jj).wait_send())
-    loop(NZ - 1, lambda n: a2a_copy(0, farthest(n)).wait_send())
+    remote(wb.at[1], wb.at[1], wss.at[0], wrs.at[0], sib).wait_send()
+    a2a_all(0).wait_send()
     for i in relayed:
         pl.when(passes(i))(lambda i=i: pass_copy(i).wait_send())
     swap_context(0).wait_send()
@@ -405,15 +410,11 @@
             final(c, j).start()
 
     residual.wait_send()
-    loop(NZ, lambda n: (a2a_copy(1, n).wait_send(), square_copy(n, 0).wait_send(), square_copy(n, 1).wait_send()))
+    a2a_all(1).wait_send()
+    squares_all().wait_send()
     swap_context(1).wait_send()
     chain_sent(1)
-    for c in range(2):
-        for j in range(NSUB):
-            cols = pl.ds(j * TILE, TILE)
-            remote(
-                fsb.at[c, :, cols], frb.at[c, :, cols], fss.at[c, j], frs.at[c, j], (nxt, z * 2 + c)
-            ).wait_recv()
+    finals.wait_recv()
     got = [frb[c].astype(F32) for c in range(2)]
     pieces = []
     for jj in range(NZ):
@@ -422,9 +423,7 @@
             v = got[c][8 * h : 8 * h + 8, j * TILE : (j + 1) * TILE]
             pieces.append(pltpu.roll(v, 4, 0) if jj % 2 else v)
     out[0] = jnp.concatenate(pieces, axis=1)[0:4].astype(BF16)
-    for c in range(2):
-        for j in range(NSUB):
-            final(c, j).wait_send()
+    finals.wait_send()
 
 
 def per_device(hidden, norm_gain, q_gain, out_weight, positions):
@@ -455,7 +454,7 @@
             pltpu.VMEM((NZ, 16, HALF), F32),
             pltpu.VMEM((2, 8, 2, 16, HALF), BF16),
             pltpu.VMEM((2, 8, 2, 16, HALF), BF16),
-            pltpu.VMEM((1, TOK), F32),
+            pltpu.VMEM((2 * NZ, 1, TOK), F32),
             pltpu.VMEM((2 * NZ, 1, TOK), F32),
             pltpu.VMEM((16, HALF), BF16),
             pltpu.VMEM((16, HALF), BF16),
@@ -463,23 +462,23 @@
             pltpu.VMEM((2, 16, 1024), BF16),
             pltpu.VMEM((7, 16, HEAD), BF16),
             dma((4,)),
-            dma((NZ,)),
-            dma((NZ,)),
-            dma((NZ,)),
+            dma((4,)),
+            dma((1,)),
+            dma((4,)),
             dma((5,)),
             dma((5,)),
-            dma((2, NZ)),
-            dma((2, NZ)),
             dma((2,)),
             dma((2,)),
-            dma((2, 8, 2, NSUB)),
-            dma((2, 8, 2, NSUB)),
-            dma((2, NSUB)),
-            dma((2, NSUB)),
+            dma((2,)),
+            dma((2,)),
+            dma((2, 2)),
+            dma((2, 8, 2, 2)),
+            dma((1,)),
+            dma((1,)),
             dma((7,)),
             dma((7,)),
-            dma((2 * NZ,)),
-            dma((2 * NZ,)),
+            dma((1,)),
+            dma((1,)),
         ],
         compiler_params=pltpu.CompilerParams(
             collective_id=0, has_side_effects=True, vmem_limit_bytes=60 * 1024 * 1024

time: 91.4 us -> 87.6 us (0.958)
  Pallas kernels: 89.7 us -> 86 us
    pallas_call x1, Pallas kernels: 89.7 us -> 86 us  [per_device(): pl.pallas_call(kernel, out_shape=jax.ShapeDtypeStruct(hidden.shape, BF16)...]
where the time goes in v4:
time: 87.6 us; the launch traced here: 87.5 us
  Pallas kernels  86 us (98%)
  local copies, waits for them, and re-layouts  1.49 us (2%)
    pallas_call x1, Pallas kernels, per_device(): pl.pallas_call(kernel, out_shape=jax.ShapeDtypeStruct(hidden.shape, BF16)...  86 us

profile of v4, /device:TPU:1, one launch (start us, length us, event | category | flops | bytes accessed | tf_op | source)
XLA Modules:
  0.0 87.5 jit_solution(7778911965926016284)
XLA Ops:
  0.0 86.0 %shard_map.55 = bf16[1,4,8192]{2,1,0:T(4,128)(2,1)} custom-call(bf16[1,4,8192]{2,1,0:T(4,128)(2,1)} %hidden_hbm.1, f32[1,8192]{1,0:T(1,128)} %gain_hbm.1, f32[1,8192]{1,0:T(1,128)} %qgain_hbm.1, bf16[1,256,8192]{2,1,0:T(8,128)(2,1)} %weight.1, s32[1,128]{1,0:T(1,128)} %pos_hbm.1), custom_call_target="tpu_custom_call" | custom-call | tf_op jit(solution)/shard_map/pallas_call | solution.py:432
  86.0 1.5 %copy.7 = bf16[1,4,8192]{2,1,0:T(4,128)(2,1)} copy(bf16[1,4,8192]{2,1,0:T(4,128)(2,1)} %shard_map.55) | data formatting | bytes 131072

commit v5 on v4

--- a/solution.py
+++ b/solution.py
@@ -20,7 +20,7 @@
 NSUB = 4
 PART = HALF // NSUB
 AHEAD = 3
-EARLY = 6
+EARLY = 4
 NEAR = 4
 
 
@@ -357,9 +357,8 @@
         wide = jnp.concatenate([back[b * 16 : (b + 1) * 16] for b in range(n)], axis=1)
         return (st[...] + wide).astype(BF16)
 
-    def final(c, j):
-        cols = pl.ds(j * TILE, TILE)
-        return remote(fsb.at[c, :, cols], frb.at[k, :, cols], fss.at[0], frs.at[0], (nxt, z * 2 + c))
+    def final(c):
+        return remote(fsb.at[c], frb.at[k], fss.at[0], frs.at[0], (nxt, z * 2 + c))
 
     finals = remote(fsb, frb, fss.at[0], frs.at[0], sib)
 
@@ -405,9 +404,8 @@
         pair = [swap(v[8 * h : 8 * h + 8, 0:TILE], v[8 * h : 8 * h + 8, TILE:PART]) for h in range(2)]
         for c in range(2):
             fsb[c, :, j * TILE : (j + 1) * TILE] = jnp.concatenate([pair[0][c], pair[1][c]], axis=0).astype(BF16)
-    for j in range(NSUB):
-        for c in range(2):
-            final(c, j).start()
+    for c in range(2):
+        final(c).start()
 
     residual.wait_send()
     a2a_all(1).wait_send()

time: 87.6 us -> 87.3 us (level)
  no operation moved by 1% of the time
where the time goes in v5:
time: 87.3 us; the launch traced here: 87.1 us
  Pallas kernels  85.6 us (98%)
  local copies, waits for them, and re-layouts  1.49 us (2%)
    pallas_call x1, Pallas kernels, per_device(): pl.pallas_call(kernel, out_shape=jax.ShapeDtypeStruct(hidden.shape, BF16)...  85.6 us

profile of v5, /device:TPU:1, one launch (start us, length us, event | category | flops | bytes accessed | tf_op | source)
XLA Modules:
  0.0 87.1 jit_solution(2363284534789472205)
XLA Ops:
  0.0 85.6 %shard_map.55 = bf16[1,4,8192]{2,1,0:T(4,128)(2,1)} custom-call(bf16[1,4,8192]{2,1,0:T(4,128)(2,1)} %hidden_hbm.1, f32[1,8192]{1,0:T(1,128)} %gain_hbm.1, f32[1,8192]{1,0:T(1,128)} %qgain_hbm.1, bf16[1,256,8192]{2,1,0:T(8,128)(2,1)} %weight.1, s32[1,128]{1,0:T(1,128)} %pos_hbm.1), custom_call_target="tpu_custom_call" | custom-call | tf_op jit(solution)/shard_map/pallas_call | solution.py:430
  85.6 1.5 %copy.7 = bf16[1,4,8192]{2,1,0:T(4,128)(2,1)} copy(bf16[1,4,8192]{2,1,0:T(4,128)(2,1)} %shard_map.55) | data formatting | bytes 131072
